TPU v7x, 32 devices: a whole 2x2x4 slice. The times are simulated.
32 devices in a mesh: groups: 2 (over y), row: 4 (over z), col: 2 (over x), sub: 2 (over core).
Axes of the slice: x: 2, y: 2, z: 4, core: 2. Of those that a mesh axis runs over, the one named last changes fastest.
Arguments:
- density: bfloat16 [4096, 2048], P(('groups', 'row'), ('col', 'sub')), parts along dimension 0, as said below
- margin: bfloat16 [4096, 2048], P(('groups', 'row'), ('col', 'sub')), parts along dimension 0, as said below
- pattern_d: int32 [32, 16], P(('groups', 'row'), ('col', 'sub')), parts along dimension 0, may hold values from 0 to 1, as said below
- pattern_s: int32 [32, 16], P(('groups', 'row'), ('col', 'sub')), parts along dimension 0, may hold values from 0 to 1, as said below
- dipole: bfloat16 [3, 4096], P(None, ('groups', 'col', 'sub')), parts along dimension 1, may hold values from -0.125 to 0.125
- owner: int32 [3, 32768], P(None, ('groups', 'row', 'col', 'sub')), parts along dimension 1, may hold values from 0 to 2047
- centres: float32 [3, 32768], P(None, ('groups', 'row', 'col', 'sub')), parts along dimension 1, may hold values from 0 to 3
- angles: float32 [3, 32768], P(None, ('groups', 'row', 'col', 'sub')), parts along dimension 1, may hold values from -3.140625 to 3.140625
- velocity: float32 [3, 32768], P(None, ('groups', 'row', 'col', 'sub')), parts along dimension 1, may hold values from -6 to 6
- angmom: float32 [3, 32768], P(None, ('groups', 'row', 'col', 'sub')), parts along dimension 1, may hold values from -6 to 6
- halo_list: int32 [2, 8192], P(None, ('groups', 'row', 'col', 'sub')), parts along dimension 1, may hold values from 0 to 1023
- neighbours: int32 [32, 32768], P(None, ('groups', 'row', 'col', 'sub')), parts along dimension 1, may hold values from 0 to 1535
Outputs:
- qm_out: bfloat16 [4096, 2048], P(('groups', 'row'), ('col', 'sub')), parts along dimension 0
- centres_new: float32 [3, 32768], P(None, ('groups', 'row', 'col', 'sub')), parts along dimension 1
- velocity_new: float32 [3, 32768], P(None, ('groups', 'row', 'col', 'sub')), parts along dimension 1
- angmom_new: float32 [3, 32768], P(None, ('groups', 'row', 'col', 'sub')), parts along dimension 1
- orient_new: float32 [4, 32768], P(None, ('groups', 'row', 'col', 'sub')), parts along dimension 1
There are 2 independent parts, one for each index of `groups`. A program takes and returns all parts, laid end to end along the dimension named above; each array names one. Nothing has to cross between parts.
Inputs may be any that keep to these rules, and one draw needn't show every extreme that they name: density is symmetric. margin is symmetric. `pattern_d`: symmetric, ones on the diagonal. `pattern_s`: every block row holds exactly 1 ones in each aligned run of 4 block columns.
All inputs are finite; a program needn't handle non-finite values.
Results may differ from a plain program's by a relative error of at most 0.0075.
Values may be sent and summed in bfloat16 or wider, within the bound.
A program may use at most 128 MiB of HBM per device.

v0:
```python
import jax
import jax.numpy as jnp
from jax import lax
from jax.experimental import pallas as pl
from jax.experimental.pallas import tpu as pltpu
from jax.sharding import PartitionSpec as P

BLOCK = 128
UNIT = 0.417
OFFSET = ((0.0, 0.0, -0.12), (0.76, 0.0, 0.47), (-0.76, 0.0, 0.47))
WEIGHT = (-2.0, 1.0, 1.0)
CHARGE = (-0.834, 0.417, 0.417)
COUPLE = 0.1
STEP_DT = 0.5
WATER_MASS = 1.0
INERTIA = 0.5
SOFTEN = 1.0
CHUNKS = 4
F32 = jnp.float32
BF16 = jnp.bfloat16


def lookup(row, low):
    return jnp.take_along_axis(
        jnp.broadcast_to(row, low.shape), low, axis=1, mode="promise_in_bounds"
    )


def dense(ref, compo):
    count = ref.shape[1] // BLOCK
    return jnp.concatenate(
        [ref[compo : compo + 1, j * BLOCK : (j + 1) * BLOCK] for j in range(count)], axis=0
    )


def spread(ref, compo, value):
    for j in range(ref.shape[1] // BLOCK):
        ref[compo : compo + 1, j * BLOCK : (j + 1) * BLOCK] = value[j : j + 1, :]


def cross(a, b):
    return (
        a[1] * b[2] - a[2] * b[1],
        a[2] * b[0] - a[0] * b[2],
        a[0] * b[1] - a[1] * b[0],
    )


def quaternion(angles):
    cos_r, cos_p, cos_y = [jnp.cos(0.5 * a) for a in angles]
    sin_r, sin_p, sin_y = [jnp.sin(0.5 * a) for a in angles]
    return (
        cos_r * cos_p * cos_y + sin_r * sin_p * sin_y,
        sin_r * cos_p * cos_y - cos_r * sin_p * sin_y,
        cos_r * sin_p * cos_y + sin_r * cos_p * sin_y,
        cos_r * cos_p * sin_y - sin_r * sin_p * cos_y,
    )


def rotation(quat):
    w, x, y, z = quat
    return (
        (1.0 - 2.0 * (y * y + z * z), 2.0 * (x * y - w * z), 2.0 * (x * z + w * y)),
        (2.0 * (x * y + w * z), 1.0 - 2.0 * (x * x + z * z), 2.0 * (y * z - w * x)),
        (2.0 * (x * z - w * y), 2.0 * (y * z + w * x), 1.0 - 2.0 * (x * x + y * y)),
    )


def make_kernel(n_row, n_col, n_sub, rows, cols, waters, neigh, halo):
    n_m = n_col * n_sub
    order = rows * n_row
    rb, cb, nb = rows // BLOCK, cols // BLOCK, order // BLOCK
    wt, nh = waters // BLOCK, halo // BLOCK
    step = rows // CHUNKS
    per = wt // CHUNKS

    def kernel(
        density, margin, pat_d, pat_s, dipole, owner, centres, angles, velocity, angmom,
        halo_list, neighbours,
        qm_out, centres_new, velocity_new, angmom_new, orient_new,
        panel, comp, full, hist1, hist2, halo_out, halo_in, field1, field2,
        table, force, quats, potential, coupled,
        d_send, d_recv, f_send, s_send, s_recv, h_send, h_recv, p_send, p_recv,
        g_send, g_recv, e_send, e_recv, q_send, q_recv, o_sem,
    ):
        row, col, sub = lax.axis_index("row"), lax.axis_index("col"), lax.axis_index("sub")
        me = col * n_sub + sub

        def peer(dc, du):
            return {"col": lax.rem(col + dc, n_col), "sub": lax.rem(sub + du, n_sub)}

        def peer_row(dr):
            return {"row": lax.rem(row + dr, n_row)}

        def source(dc, du):
            return (
                lax.rem(col + n_col - dc, n_col) * n_sub + lax.rem(sub + n_sub - du, n_sub)
            )

        pairs = [(dc, du) for dc in range(n_col) for du in range(n_sub) if dc + du > 0]
        started = []

        def send(src, dst, ssem, rsem, dev):
            copy = pltpu.make_async_remote_copy(
                src_ref=src, dst_ref=dst, send_sem=ssem, recv_sem=rsem,
                device_id=dev, device_id_type=pl.DeviceIdType.MESH,
            )
            copy.start()
            return copy

        barrier = pltpu.get_barrier_semaphore()
        for dc, du in pairs:
            pl.semaphore_signal(
                barrier, inc=1, device_id=peer(dc, du), device_id_type=pl.DeviceIdType.MESH
            )
        for dr in range(1, n_row):
            pl.semaphore_signal(
                barrier, inc=1, device_id=peer_row(dr), device_id_type=pl.DeviceIdType.MESH
            )

        for i in range(rb):
            at = slice(i * BLOCK, (i + 1) * BLOCK)
            total = None
            for j in range(cb):
                ac = slice(j * BLOCK, (j + 1) * BLOCK)
                factor = pat_d[i, j].astype(F32)
                panel[me, at, ac] = (density[at, ac].astype(F32) * factor).astype(BF16)
                term = margin[at, ac].astype(F32) * pat_s[i, j].astype(F32)
                total = term if total is None else total + term
            comp[row, at, :] = total.astype(BF16)
        for base in range(0, rb * cb, 16):
            comp[row, rows + base : rows + base + 16, :] = jnp.concatenate(
                [
                    jnp.full((1, BLOCK), pat_s[q // cb, q % cb].astype(F32), F32)
                    for q in range(base, base + 16)
                ],
                axis=0,
            ).astype(BF16)

        lane_ids = lax.broadcasted_iota(jnp.int32, (BLOCK, waters), 0)
        high_ids = lax.broadcasted_iota(jnp.int32, (nb, waters), 0)
        counts = jnp.zeros((nb, BLOCK), F32)
        for site in range(3):
            own = owner[site : site + 1, :]
            low_hot = jnp.where(lane_ids == (own & (BLOCK - 1)), 1.0, 0.0).astype(BF16)
            high_hot = jnp.where(high_ids == (own >> 7), WEIGHT[site], 0.0).astype(BF16)
            counts = counts + lax.dot_general(
                high_hot, low_hot, (((1,), (1,)), ((), ())), preferred_element_type=F32
            )
        hist1[0] = counts
        cent = [dense(centres, c) for c in range(3)]
        quat = quaternion([dense(angles, c) for c in range(3)])
        for c in range(4):
            quats[c] = quat[c]
        matrix = rotation(quat)
        for a in range(3):
            for c in range(3):
                table[3 * a + c] = (
                    cent[c]
                    + matrix[c][0] * OFFSET[a][0]
                    + matrix[c][1] * OFFSET[a][1]
                    + matrix[c][2] * OFFSET[a][2]
                )
        listed = [
            halo_list[side : side + 1, j * BLOCK : (j + 1) * BLOCK]
            for side in range(2) for j in range(nh)
        ]
        picks = jnp.concatenate(listed + [listed[0]] * (8 - len(listed)), axis=0)
        low, high = picks & (BLOCK - 1), picks >> 7
        for t in range(9):
            value = lookup(table[t, 0:1, :], low)
            for h in range(1, wt):
                value = jnp.where(high == h, lookup(table[t, h : h + 1, :], low), value)
            for side in range(2):
                halo_out[side, t * nh : (t + 1) * nh, :] = value[side * nh : (side + 1) * nh, :]
        pl.semaphore_wait(barrier, len(pairs) + n_row - 1)

        for n, (dc, du) in enumerate(pairs):
            started.append(
                send(hist1.at[0], hist1.at[n + 1], h_send.at[n], h_recv.at[n], peer(dc, du))
            )

        for side, by in ((0, 1), (1, n_row - 1)):
            started.append(
                send(halo_out.at[side], halo_in.at[side], e_send.at[side], e_recv.at[side],
                     peer_row(by))
            )

        for k in range(CHUNKS):
            at = pl.ds(k * step, step)
            for dc in range(1, n_col):
                started.append(
                    send(panel.at[me, at], panel.at[me, at], d_send.at[dc, 0, k],
                         d_recv.at[dc, 0, k], peer(dc, 0))
                )
        def relay_send(way, t):
            block = lax.rem(row + n_row - t, n_row) if way == 0 else lax.rem(row + t, n_row)
            return pltpu.make_async_remote_copy(
                src_ref=comp.at[block], dst_ref=comp.at[block], send_sem=s_send.at[way, t],
                recv_sem=s_recv.at[way, t], device_id=peer_row(1 if way == 0 else n_row - 1),
                device_id_type=pl.DeviceIdType.MESH,
            )

        ahead = (row + 1 < n_row, row >= 1)

        def held_back(way, t):
            return row - t >= 0 if way == 0 else row + t < n_row

        for way in range(2):
            pl.when(ahead[way])(lambda way=way: relay_send(way, 0).start())
        for k in range(CHUNKS):
            at = pl.ds(k * step, step)
            for du in range(1, n_sub):
                started.append(
                    send(panel.at[me, at], panel.at[me, at], d_send.at[0, du, k],
                         d_recv.at[0, du, k], peer(0, du))
                )

        def arrived(ref, sem):
            pltpu.make_async_copy(ref, ref, sem).wait()

        for n in range(len(pairs)):
            arrived(hist1.at[n + 1], h_recv.at[n])
        counts = hist1[0]
        for n in range(len(pairs)):
            counts = counts + hist1[n + 1]
        hist2[0] = counts
        for dr in range(1, n_row):
            started.append(
                send(hist2.at[0], hist2.at[dr], p_send.at[dr], p_recv.at[dr], peer_row(dr))
            )
        for side in range(2):
            arrived(halo_in.at[side], e_recv.at[side])

        def expand(r, _):
            marks = comp[r, rows : rows + rb * cb, :].astype(F32)
            for i in range(rb):
                tile = comp[r, i * BLOCK : (i + 1) * BLOCK, :].astype(F32)
                at = pl.ds(pl.multiple_of(r * rows + i * BLOCK, BLOCK), BLOCK)
                for j in range(cb):
                    q = i * cb + j
                    full[at, j * BLOCK : (j + 1) * BLOCK] = (tile * marks[q : q + 1, :]).astype(BF16)
            return 0

        def relay(t):
            for way in range(2):
                @pl.when(held_back(way, t))
                def _(way=way):
                    block = lax.rem(row + n_row - t, n_row) if way == 0 else lax.rem(row + t, n_row)
                    arrived(comp.at[block], s_recv.at[way, t - 1])
                    pl.when(ahead[way])(lambda: relay_send(way, t).start())
                    expand(block, 0)

        expand(row, 0)

        def pair_tile(j):
            lanes = pl.ds(pl.multiple_of(j * BLOCK, BLOCK), BLOCK)
            own = [jnp.broadcast_to(table[t, pl.ds(j, 1), :], (8, BLOCK)) for t in range(9)]
            totals = [jnp.zeros((8, BLOCK), F32) for _ in range(9)]
            for s in range(0, neigh, 8):
                idx = neighbours[s : s + 8, lanes]
                low, high = idx & (BLOCK - 1), idx >> 7
                part = [lookup(table[t, 0:1, :], low) for t in range(9)]
                for h in range(1, wt + 2 * nh):
                    hit = high == h
                    for t in range(9):
                        if h < wt:
                            line = table[t, h : h + 1, :]
                        else:
                            side, at = (h - wt) // nh, t * nh + (h - wt) % nh
                            line = halo_in[side, at : at + 1, :]
                        part[t] = jnp.where(hit, lookup(line, low), part[t])
                for a in range(3):
                    for b in range(3):
                        d = [own[3 * a + c] - part[3 * b + c] for c in range(3)]
                        inv = lax.rsqrt(d[0] * d[0] + d[1] * d[1] + d[2] * d[2] + SOFTEN)
                        weight = (CHARGE[a] * CHARGE[b]) * (inv * inv * inv)
                        for c in range(3):
                            totals[3 * a + c] = totals[3 * a + c] + d[c] * weight
            for t in range(9):
                force[t, pl.ds(j, 1), :] = jnp.sum(totals[t], axis=0, keepdims=True)

        def pair_and_pass(k, _):
            lax.fori_loop(0, per, lambda i, c: (pair_tile(k * per + i), c)[1], 0)
            at = pl.ds(pl.multiple_of(k * step, step), step)
            for dc in range(1, n_col):
                slot = source(dc, 0)
                arrived(panel.at[slot, at], d_recv.at[dc, 0, k])
                for du in range(1, n_sub):
                    send(panel.at[slot, at], panel.at[slot, at], f_send.at[dc, du, k],
                         d_recv.at[dc, du, k], peer(0, du))
            relay(k + 1)
            return 0

        lax.fori_loop(0, CHUNKS, pair_and_pass, 0)

        for dr in range(1, n_row):
            arrived(hist2.at[dr], p_recv.at[dr])
        counts = hist2[0]
        for dr in range(1, n_row):
            counts = counts + hist2[dr]
        potential[...] = counts * UNIT

        lax.fori_loop(CHUNKS + 1, n_row, lambda t, c: (relay(t), c)[1], 0)
        col_pot = jnp.concatenate(
            [potential[pl.ds(me * cb + j, 1), :] for j in range(cb)], axis=1
        )
        eye = (
            lax.broadcasted_iota(jnp.int32, (BLOCK, BLOCK), 0)
            == lax.broadcasted_iota(jnp.int32, (BLOCK, BLOCK), 1)
        )

        def product(k, _):
            at = pl.ds(pl.multiple_of(k * step, step), step)
            total = jnp.zeros((step, cols), F32)
            for dc in range(n_col):
                for du in range(n_sub):
                    slot = source(dc, du)
                    if (dc, du) != (0, 0) and not (dc > 0 and du == 0):
                        arrived(panel.at[slot, at], d_recv.at[dc, du, k])
                    depth = pl.ds(pl.multiple_of(slot * cols, cols), cols)
                    total = total + jnp.dot(
                        panel[slot, at, :], full[depth, :], preferred_element_type=F32
                    )
            line = potential[pl.ds(row * rb + k, 1), :]
            row_pot = jnp.sum(jnp.where(eye, line, 0.0), axis=1, keepdims=True)
            mine = panel[me, at, :].astype(F32)
            out = (total + COUPLE * (row_pot + col_pot) * mine).astype(BF16)
            coupled[at, :] = out
            pltpu.make_async_copy(coupled.at[at], qm_out.at[at], o_sem.at[k]).start()
            part = lax.dot_general(
                dipole[...], out, (((1,), (1,)), ((), ())), preferred_element_type=F32
            )
            for c in range(3):
                field1[0, pl.ds(4 * k + c, 1), :] = part[c : c + 1, :]
            return 0

        lax.fori_loop(0, CHUNKS, product, 0)

        for n, (dc, du) in enumerate(pairs):
            started.append(
                send(field1.at[0], field1.at[n + 1], g_send.at[n], g_recv.at[n], peer(dc, du))
            )
        for n in range(len(pairs)):
            arrived(field1.at[n + 1], g_recv.at[n])
        total = field1[0]
        for n in range(len(pairs)):
            total = total + field1[n + 1]
        field2[row] = total
        for dr in range(1, n_row):
            started.append(
                send(field2.at[row], field2.at[row], q_send.at[dr], q_recv.at[dr], peer_row(dr))
            )
        for dr in range(1, n_row):
            arrived(field2.at[lax.rem(row + n_row - dr, n_row)], q_recv.at[dr])

        forces = []
        for a in range(3):
            own = dense(owner, a)
            low, high = own & (BLOCK - 1), own >> 7
            value = [jnp.zeros((wt, BLOCK), F32)] * 3
            for h in range(nb):
                hit = high == h
                at = 4 * (h % rb)
                for c in range(3):
                    value[c] = jnp.where(
                        hit, lookup(field2[h // rb, at + c : at + c + 1, :], low), value[c]
                    )
            forces.append([force[3 * a + c] + CHARGE[a] * value[c] for c in range(3)])
        cent = [dense(centres, c) for c in range(3)]
        quat = [quats[c] for c in range(4)]
        torque = [jnp.zeros((wt, BLOCK), F32)] * 3
        for a in range(3):
            lever = [table[3 * a + c] - cent[c] for c in range(3)]
            turn = cross(lever, forces[a])
            torque = [torque[c] + turn[c] for c in range(3)]
        omega = []
        for c in range(3):
            pull = forces[0][c] + forces[1][c] + forces[2][c]
            fast = dense(velocity, c) + STEP_DT * pull / WATER_MASS
            spread(velocity_new, c, fast)
            spread(centres_new, c, cent[c] + STEP_DT * fast)
            spin = dense(angmom, c) + STEP_DT * torque[c]
            spread(angmom_new, c, spin)
            omega.append(spin / INERTIA)
        vector = quat[1:4]
        delta = [-(omega[0] * vector[0] + omega[1] * vector[1] + omega[2] * vector[2])]
        turn = cross(omega, vector)
        delta += [quat[0] * omega[c] + turn[c] for c in range(3)]
        moved = [quat[c] + 0.5 * STEP_DT * delta[c] for c in range(4)]
        length = jnp.sqrt(sum(m * m for m in moved))
        for c in range(4):
            spread(orient_new, c, moved[c] / length)

        for k in range(CHUNKS):
            at = pl.ds(k * step, step)
            pltpu.make_async_copy(coupled.at[at], qm_out.at[at], o_sem.at[k]).wait()
        for way in range(2):
            for t in range(n_row - 1):
                @pl.when(jnp.logical_and(ahead[way], held_back(way, t)))
                def _(way=way, t=t):
                    relay_send(way, t).wait_send()
        for copy in started:
            copy.wait_send()
        for k in range(CHUNKS):
            at = pl.ds(k * step, step)
            for dc in range(1, n_col):
                for du in range(1, n_sub):
                    arrived(panel.at[source(dc, 0), at], f_send.at[dc, du, k])

    vmem = pl.BlockSpec(memory_space=pltpu.VMEM)
    smem = pl.BlockSpec(memory_space=pltpu.SMEM)
    dma = lambda *s: pltpu.SemaphoreType.DMA(s)
    extra = n_m - 1
    call = pl.pallas_call(
        kernel,
        out_shape=(
            jax.ShapeDtypeStruct((rows, cols), BF16),
            jax.ShapeDtypeStruct((3, waters), F32),
            jax.ShapeDtypeStruct((3, waters), F32),
            jax.ShapeDtypeStruct((3, waters), F32),
            jax.ShapeDtypeStruct((4, waters), F32),
        ),
        in_specs=[vmem, vmem, smem, smem] + [vmem] * 8,
        out_specs=(pl.BlockSpec(memory_space=pl.ANY),) + (vmem,) * 4,
        scratch_shapes=[
            pltpu.VMEM((n_m, rows, cols), BF16),
            pltpu.VMEM((n_row, rows + rb * cb, BLOCK), BF16),
            pltpu.VMEM((order, cols), BF16),
            pltpu.VMEM((n_m, nb, BLOCK), F32),
            pltpu.VMEM((n_row, nb, BLOCK), F32),
            pltpu.VMEM((2, 24, BLOCK), F32),
            pltpu.VMEM((2, 24, BLOCK), F32),
            pltpu.VMEM((n_m, rb * 4, BLOCK), F32),
            pltpu.VMEM((n_row, rb * 4, BLOCK), F32),
            pltpu.VMEM((9, wt, BLOCK), F32),
            pltpu.VMEM((9, wt, BLOCK), F32),
            pltpu.VMEM((4, wt, BLOCK), F32),
            pltpu.VMEM((nb, BLOCK), F32),
            pltpu.VMEM((rows, cols), BF16),
            dma(n_col, n_sub, CHUNKS), dma(n_col, n_sub, CHUNKS), dma(n_col, n_sub, CHUNKS),
            dma(2, n_row), dma(2, n_row), dma(extra), dma(extra), dma(n_row), dma(n_row),
            dma(extra), dma(extra), dma(2), dma(2), dma(n_row), dma(n_row),
            dma(CHUNKS),
        ],
        compiler_params=pltpu.CompilerParams(
            collective_id=0, has_side_effects=True, vmem_limit_bytes=56 << 20
        ),
    )
    return call


def deliver(results):
    count = len(results)

    pieces = [
        (n, k * (r.shape[0] // parts), r.shape[0] // parts)
        for n, r in enumerate(results)
        for parts in ((CHUNKS if n == 0 else 1),)
        for k in range(parts)
    ]

    def kernel(*refs):
        held = refs[2 * count : 3 * count]
        in_sem, out_sem = refs[3 * count :]
        loads, stores = [], []
        for q, (n, at, size) in enumerate(pieces):
            part = pl.ds(at, size)
            loads.append(
                pltpu.make_async_copy(refs[n].at[part], held[n].at[part], in_sem.at[q])
            )
            stores.append(
                pltpu.make_async_copy(held[n].at[part], refs[count + n].at[part], out_sem.at[q])
            )
        for load in loads:
            load.start()
        for load, store in zip(loads, stores):
            load.wait()
            store.start()
        for store in stores:
            store.wait()

    anywhere = pl.BlockSpec(memory_space=pl.ANY)
    return pl.pallas_call(
        kernel,
        out_shape=tuple(jax.ShapeDtypeStruct(r.shape, r.dtype) for r in results),
        in_specs=[anywhere] * count,
        out_specs=(anywhere,) * count,
        scratch_shapes=[pltpu.VMEM(r.shape, r.dtype) for r in results]
        + [pltpu.SemaphoreType.DMA((len(pieces),))] * 2,
    )(*results)


def solution(mesh):
    n_row, n_col, n_sub = mesh.shape["row"], mesh.shape["col"], mesh.shape["sub"]

    def shards(density, margin, pattern_d, pattern_s, dipole, owner, centres, angles,
               velocity, angmom, halo_list, neighbours):
        call = make_kernel(
            n_row, n_col, n_sub, density.shape[0], density.shape[1], owner.shape[1],
            neighbours.shape[0], halo_list.shape[1],
        )
        return deliver(
            call(density, margin, pattern_d, pattern_s, dipole, owner, centres, angles,
                 velocity, angmom, halo_list, neighbours)
        )

    block = P(("groups", "row"), ("col", "sub"))
    water = P(None, ("groups", "row", "col", "sub"))
    return jax.shard_map(
        shards,
        mesh=mesh,
        in_specs=(block,) * 4 + (P(None, ("groups", "col", "sub")),) + (water,) * 7,
        out_specs=(block,) + (water,) * 4,
        check_vma=False,
    )
```

profile of v0, /device:TPU:0, one launch (start us, length us, event | category | flops | bytes accessed | tf_op | source)
XLA Modules:
  0.0 34.6 jit_solution(16085431046150994882)
XLA Ops:
  0.6 32.0 %shard_map.155 = (bf16[512,512]{1,0:T(8,128)(2,1)}, f32[3,1024]{1,0:T(4,128)}, f32[3,1024]{1,0:T(4,128)}, f32[3,1024]{1,0:T(4,128)}, f32[4,1024]{1,0:T(4,128)}) custom-call(bf16[512,512]{1,0:T(8,128)(2,1)} %density.1, bf16[512,512]{1,0:T(8,128)(2,1)} %margin.1, s32[4,4]{1,0:T(4,128)} %pat_d.1, s32[4,4]{1,0:T(4,128)} %pat_s.1, bf16[3,512]{1,0:T(4,128)(2,1)} %dipole.1, ...), custom_call_target="tpu_custom_call" | custom-call | tf_op jit(solution)/shard_map/pallas_call | solution.py:504
  32.7 1.9 %shard_map.156 = (bf16[512,512]{1,0:T(8,128)(2,1)}, f32[3,1024]{1,0:T(4,128)}, f32[3,1024]{1,0:T(4,128)}, f32[3,1024]{1,0:T(4,128)}, f32[4,1024]{1,0:T(4,128)}) custom-call(bf16[512,512]{1,0:T(8,128)(2,1)} %get-tuple-element.10.refs_0_, f32[3,1024]{1,0:T(4,128)} %get-tuple-element.11.refs_1_, f32[3,1024]{1,0:T(4,128)} %get-tuple-element.12.refs_2_, ...), custom_call_target="tpu_custom_call" | custom-call | tf_op jit(solution)/shard_map/pallas_call | solution.py:484
where the time goes:
time: 34.7 us; the launch traced here: 34.6 us
  Pallas kernels  33.9 us (98%)
  between operations  0.64 us (2%)
    pallas_call x1, Pallas kernels, shards(): call(density, margin, pattern_d, pattern_s, dipole, owner, centres, angle...  32 us
    pallas_call x1, Pallas kernels, deliver(): pl.pallas_call(kernel, out_shape=tuple((jax.ShapeDtypeStruct(r.shape, r.d...  1.9 us

commit v1 on v0

v1 whole, which is shorter than its diff:
```python
import jax
import jax.numpy as jnp
from jax import lax
from jax.experimental import pallas as pl
from jax.experimental.pallas import tpu as pltpu
from jax.sharding import PartitionSpec as P

BLOCK = 128
UNIT = 0.417
OFFSET = ((0.0, 0.0, -0.12), (0.76, 0.0, 0.47), (-0.76, 0.0, 0.47))
WEIGHT = (-2.0, 1.0, 1.0)
CHARGE = (-0.834, 0.417, 0.417)
COUPLE = 0.1
STEP_DT = 0.5
WATER_MASS = 1.0
INERTIA = 0.5
SOFTEN = 1.0
CHUNKS = 4
F32 = jnp.float32
BF16 = jnp.bfloat16


def lookup(row, low):
    return jnp.take_along_axis(
        jnp.broadcast_to(row, low.shape), low, axis=1, mode="promise_in_bounds"
    )


def dense(ref, compo):
    count = ref.shape[1] // BLOCK
    return jnp.concatenate(
        [ref[compo : compo + 1, j * BLOCK : (j + 1) * BLOCK] for j in range(count)], axis=0
    )


def spread(ref, compo, value):
    for j in range(ref.shape[1] // BLOCK):
        ref[compo : compo + 1, j * BLOCK : (j + 1) * BLOCK] = value[j : j + 1, :]


def cross(a, b):
    return (
        a[1] * b[2] - a[2] * b[1],
        a[2] * b[0] - a[0] * b[2],
        a[0] * b[1] - a[1] * b[0],
    )


def quaternion(angles):
    cos_r, cos_p, cos_y = [jnp.cos(0.5 * a) for a in angles]
    sin_r, sin_p, sin_y = [jnp.sin(0.5 * a) for a in angles]
    return (
        cos_r * cos_p * cos_y + sin_r * sin_p * sin_y,
        sin_r * cos_p * cos_y - cos_r * sin_p * sin_y,
        cos_r * sin_p * cos_y + sin_r * cos_p * sin_y,
        cos_r * cos_p * sin_y - sin_r * sin_p * cos_y,
    )


def rotation(quat):
    w, x, y, z = quat
    return (
        (1.0 - 2.0 * (y * y + z * z), 2.0 * (x * y - w * z), 2.0 * (x * z + w * y)),
        (2.0 * (x * y + w * z), 1.0 - 2.0 * (x * x + z * z), 2.0 * (y * z - w * x)),
        (2.0 * (x * z - w * y), 2.0 * (y * z + w * x), 1.0 - 2.0 * (x * x + y * y)),
    )


def make_kernel(n_row, n_col, n_sub, rows, cols, waters, neigh, halo):
    n_m = n_col * n_sub
    n_all = n_row * n_m
    order = rows * n_row
    rb, cb, nb = rows // BLOCK, cols // BLOCK, order // BLOCK
    wt, nh = waters // BLOCK, halo // BLOCK
    wide = cols // rows
    step = rows // CHUNKS
    hr = 9 * nh

    def kernel(
        density_hbm, margin_hbm, pat_d_hbm, pat_s_hbm, dipole_hbm, owner_hbm, centres_hbm,
        angles_hbm, velocity_hbm, angmom_hbm, halo_list_hbm, neighbours_hbm,
        coupled, centres_new, velocity_new, angmom_new, orient_new,
        density, margin, pat_d, pat_s, dipole, owner, centres,
        angles, velocity, angmom, halo_list, neighbours,
        panel, comp, full, hist, inner, parts, field, halo_out, halo_in,
        table, force, quats, potential, sums,
        l_sem, c_sem, d_send, d_recv, f_send, s_send, s_recv, h_send, h_recv, v_send, v_recv,
        q_send, q_recv, e_send, e_recv,
    ):
        row, col, sub = lax.axis_index("row"), lax.axis_index("col"), lax.axis_index("sub")
        me = col * n_sub + sub

        def peer(dc, du):
            return {"col": lax.rem(col + dc, n_col), "sub": lax.rem(sub + du, n_sub)}

        def peer_row(dr):
            return {"row": lax.rem(row + dr, n_row)}

        def other(q):
            dr, dm = lax.div(q, n_m), lax.rem(q, n_m)
            return {
                "row": lax.rem(row + dr, n_row),
                "col": lax.rem(col + lax.div(dm, n_sub), n_col),
                "sub": lax.rem(sub + lax.rem(dm, n_sub), n_sub),
            }

        def source(dc, du):
            return (
                lax.rem(col + n_col - dc, n_col) * n_sub + lax.rem(sub + n_sub - du, n_sub)
            )

        started = []

        def remote(src, dst, ssem, rsem, dev):
            return pltpu.make_async_remote_copy(
                src_ref=src, dst_ref=dst, send_sem=ssem, recv_sem=rsem,
                device_id=dev, device_id_type=pl.DeviceIdType.MESH,
            )

        def send(src, dst, ssem, rsem, dev):
            copy = remote(src, dst, ssem, rsem, dev)
            copy.start()
            return copy

        def arrived(ref, sem):
            pltpu.make_async_copy(ref, ref, sem).wait()

        barrier = pltpu.get_barrier_semaphore()

        def greet(q, carry):
            pl.semaphore_signal(
                barrier, inc=1, device_id=other(q), device_id_type=pl.DeviceIdType.MESH
            )
            return carry

        small = [
            pltpu.make_async_copy(src, dst, l_sem.at[n])
            for n, (src, dst) in enumerate((
                (pat_d_hbm, pat_d), (pat_s_hbm, pat_s), (dipole_hbm, dipole),
                (owner_hbm, owner), (angles_hbm, angles), (centres_hbm, centres),
                (halo_list_hbm, halo_list), (neighbours_hbm, neighbours),
                (velocity_hbm, velocity), (angmom_hbm, angmom), (margin_hbm, margin),
            ))
        ]
        loads = [
            pltpu.make_async_copy(
                density_hbm.at[pl.ds(k * step, step)], density.at[pl.ds(k * step, step)],
                c_sem.at[k],
            )
            for k in range(CHUNKS)
        ]
        small[0].start()
        loads[0].start()
        for load in loads[1:]:
            load.start()
        small[10].start()
        for load in small[1:10]:
            load.start()
        lax.fori_loop(1, n_all, greet, 0)

        small[0].wait()
        for k in range(CHUNKS):
            loads[k].wait()
            for i in range(k * step // BLOCK, (k + 1) * step // BLOCK):
                at = slice(i * BLOCK, (i + 1) * BLOCK)
                for j in range(cb):
                    ac = slice(j * BLOCK, (j + 1) * BLOCK)
                    factor = pat_d[i, j].astype(F32)
                    panel[me, at, ac] = (density[at, ac].astype(F32) * factor).astype(BF16)
        small[1].wait()
        small[2].wait()
        small[10].wait()
        low_u = []
        for i in range(rb):
            at = slice(i * BLOCK, (i + 1) * BLOCK)
            total, chosen = None, None
            for j in range(cb):
                ac = slice(j * BLOCK, (j + 1) * BLOCK)
                factor = pat_s[i, j].astype(F32)
                term = margin[at, ac].astype(F32) * factor
                dip = dipole[:, ac].astype(F32) * factor
                total = term if total is None else total + term
                chosen = dip if chosen is None else chosen + dip
            tile = total.astype(BF16)
            comp[row, at, :] = tile
            low_u.append(
                lax.dot_general(
                    chosen.astype(BF16), tile, (((1,), (1,)), ((), ())),
                    preferred_element_type=F32,
                )
            )
        for base in range(0, rb * cb, 16):
            comp[row, rows + base : rows + base + 16, :] = jnp.concatenate(
                [
                    jnp.full((1, BLOCK), pat_s[q // cb, q % cb].astype(F32), F32)
                    for q in range(base, base + 16)
                ],
                axis=0,
            ).astype(BF16)
        target, lane = lax.div(row, wide), lax.rem(row, wide)
        for i in range(rb):
            inner[4 * i : 4 * i + 3, :] = low_u[i]
            inner[4 * i + 3 : 4 * i + 4, :] = low_u[i][0:1, :]

        small[3].wait()
        lane_ids = lax.broadcasted_iota(jnp.int32, (BLOCK, waters), 0)
        high_ids = lax.broadcasted_iota(jnp.int32, (nb, waters), 0)
        counts = jnp.zeros((nb, BLOCK), F32)
        for site in range(3):
            own = owner[site : site + 1, :]
            low_hot = jnp.where(lane_ids == (own & (BLOCK - 1)), 1.0, 0.0).astype(BF16)
            high_hot = jnp.where(high_ids == (own >> 7), WEIGHT[site], 0.0).astype(BF16)
            counts = counts + lax.dot_general(
                high_hot, low_hot, (((1,), (1,)), ((), ())), preferred_element_type=F32
            )
        hist[0] = counts.astype(jnp.int32).astype(jnp.int16)
        for load in small[4:8]:
            load.wait()
        cent = [dense(centres, c) for c in range(3)]
        quat = quaternion([dense(angles, c) for c in range(3)])
        for c in range(4):
            quats[c] = quat[c]
        matrix = rotation(quat)
        for a in range(3):
            for c in range(3):
                table[3 * a + c] = (
                    cent[c]
                    + matrix[c][0] * OFFSET[a][0]
                    + matrix[c][1] * OFFSET[a][1]
                    + matrix[c][2] * OFFSET[a][2]
                )
        listed = [
            halo_list[side : side + 1, j * BLOCK : (j + 1) * BLOCK]
            for side in range(2) for j in range(nh)
        ]
        picks = jnp.concatenate(listed + [listed[0]] * (8 - len(listed)), axis=0)
        low, high = picks & (BLOCK - 1), picks >> 7
        for t in range(9):
            value = lookup(table[t, 0:1, :], low)
            for h in range(1, wt):
                value = jnp.where(high == h, lookup(table[t, h : h + 1, :], low), value)
            for side in range(2):
                halo_out[side, t * nh : (t + 1) * nh, :] = value[side * nh : (side + 1) * nh, :]
        pl.semaphore_wait(barrier, n_all - 1)

        def share(q, carry):
            remote(hist.at[0], hist.at[q], h_send, h_recv, other(q)).start()
            return carry

        lax.fori_loop(1, n_all, share, 0)

        def pass_inner(dr):
            there = peer_row(dr)
            there["col"], there["sub"] = lax.div(target, n_sub), lax.rem(target, n_sub)
            return remote(
                inner, parts.at[lane, me], v_send.at[dr], v_recv.at[lane, me], there
            )

        @pl.when(target == me)
        def _():
            parts[lane, me] = inner[...]

        pl.when(target != me)(lambda: pass_inner(0).start())
        for dr in range(1, n_row):
            pass_inner(dr).start()
        for side, by in ((0, 1), (1, n_row - 1)):
            started.append(
                send(halo_out.at[side], halo_in.at[side], e_send.at[side], e_recv.at[side],
                     peer_row(by))
            )
        for k in range(CHUNKS):
            at = pl.ds(k * step, step)
            for dc in range(1, n_col):
                started.append(
                    send(panel.at[me, at], panel.at[me, at], d_send.at[dc, 0, k],
                         d_recv.at[dc, 0, k], peer(dc, 0))
                )
            if k == 0:
                for dr in range(1, n_row):
                    started.append(
                        send(comp.at[row], comp.at[row], s_send.at[dr], s_recv.at[dr],
                             peer_row(dr))
                    )
        for k in range(CHUNKS):
            at = pl.ds(k * step, step)
            for du in range(1, n_sub):
                started.append(
                    send(panel.at[me, at], panel.at[me, at], d_send.at[0, du, k],
                         d_recv.at[0, du, k], peer(0, du))
                )

        def expand(r):
            marks = comp[r, rows : rows + rb * cb, :].astype(F32)
            for i in range(rb):
                tile = comp[r, i * BLOCK : (i + 1) * BLOCK, :].astype(F32)
                at = pl.ds(pl.multiple_of(r * rows + i * BLOCK, BLOCK), BLOCK)
                for j in range(cb):
                    q = i * cb + j
                    full[at, j * BLOCK : (j + 1) * BLOCK] = (tile * marks[q : q + 1, :]).astype(BF16)

        def pass_on(k):
            at = pl.ds(k * step, step)
            for dc in range(1, n_col):
                slot = source(dc, 0)
                arrived(panel.at[slot, at], d_recv.at[dc, 0, k])
                for du in range(1, n_sub):
                    started.append(
                        send(panel.at[slot, at], panel.at[slot, at], f_send.at[dc, du, k],
                             d_recv.at[dc, du, k], peer(0, du))
                    )

        def pair_tile(j, carry):
            lanes = pl.ds(pl.multiple_of(j * BLOCK, BLOCK), BLOCK)
            own = [jnp.broadcast_to(table[t, pl.ds(j, 1), :], (8, BLOCK)) for t in range(9)]
            totals = [jnp.zeros((8, BLOCK), F32) for _ in range(9)]
            for s in range(0, neigh, 8):
                idx = neighbours[s : s + 8, lanes]
                low, high = idx & (BLOCK - 1), idx >> 7
                part = [lookup(table[t, 0:1, :], low) for t in range(9)]
                for h in range(1, wt + 2 * nh):
                    hit = high == h
                    for t in range(9):
                        if h < wt:
                            line = table[t, h : h + 1, :]
                        else:
                            side, at = (h - wt) // nh, t * nh + (h - wt) % nh
                            line = halo_in[side, at : at + 1, :]
                        part[t] = jnp.where(hit, lookup(line, low), part[t])
                for a in range(3):
                    for b in range(3):
                        d = [own[3 * a + c] - part[3 * b + c] for c in range(3)]
                        inv = lax.rsqrt(d[0] * d[0] + d[1] * d[1] + d[2] * d[2] + SOFTEN)
                        weight = (CHARGE[a] * CHARGE[b]) * (inv * inv * inv)
                        for c in range(3):
                            totals[3 * a + c] = totals[3 * a + c] + d[c] * weight
            for t in range(9):
                force[t, pl.ds(j, 1), :] = jnp.sum(totals[t], axis=0, keepdims=True)
            return carry

        expand(row)
        for side in range(2):
            arrived(halo_in.at[side], e_recv.at[side])
        lax.fori_loop(0, wt // 2, pair_tile, 0)

        arrived(hist.at[pl.ds(1, n_all - 1)], h_recv)
        counts = lax.fori_loop(
            1, n_all, lambda q, c: c + hist[q].astype(jnp.int32), hist[0].astype(jnp.int32)
        )
        potential[...] = counts.astype(F32) * UNIT
        for s in range(wide):
            for m in range(n_m):
                is_own = jnp.logical_and(target == me, jnp.logical_and(lane == s, me == m))
                pl.when(jnp.logical_not(is_own))(
                    lambda s=s, m=m: arrived(parts.at[s, m], v_recv.at[s, m])
                )
        lines = [[], [], []]
        for s in range(wide):
            total = parts[s, 0]
            for m in range(1, n_m):
                total = total + parts[s, m]
            for i in range(rb):
                j = s * rb + i
                weigh = COUPLE * potential[pl.ds(me * cb + j, 1), :]
                dip = dipole[:, j * BLOCK : (j + 1) * BLOCK].astype(F32)
                for c in range(3):
                    lines[c].append(total[4 * i + c : 4 * i + c + 1, :] + weigh * dip[c : c + 1, :])
        vector = jnp.concatenate([jnp.concatenate(line, axis=1) for line in lines], axis=0)
        coarse = vector.astype(BF16).astype(F32)
        stack = jnp.concatenate(
            [coarse, vector - coarse, dipole[...].astype(F32), jnp.zeros((7, cols), F32)], axis=0
        ).astype(BF16)
        for i in range(rb):
            got = lax.dot_general(
                stack, panel[me, i * BLOCK : (i + 1) * BLOCK, :], (((1,), (1,)), ((), ())),
                preferred_element_type=F32,
            )
            weigh = COUPLE * potential[pl.ds(row * rb + i, 1), :]
            inner2 = got[0:3, :] + got[3:6, :] + weigh * got[6:9, :]
            low_u[i] = jnp.concatenate([inner2, jnp.zeros((1, BLOCK), F32)], axis=0)
        field[0] = jnp.concatenate(low_u, axis=0).astype(BF16)

        def tell(q, carry):
            remote(field.at[0], field.at[q], q_send, q_recv, other(q)).start()
            return carry

        lax.fori_loop(1, n_all, tell, 0)
        pass_on(0)
        lax.fori_loop(wt // 2, wt, pair_tile, 0)
        pass_on(1)

        arrived(field.at[pl.ds(1, n_all - 1)], q_recv)
        small[8].wait()
        small[9].wait()
        for dr in range(n_row):
            total = field[dr * n_m].astype(F32)
            for m in range(1, n_m):
                total = total + field[dr * n_m + m].astype(F32)
            sums[lax.rem(row + n_row - dr, n_row)] = total

        forces = []
        for a in range(3):
            own = dense(owner, a)
            low, high = own & (BLOCK - 1), own >> 7
            value = [jnp.zeros((wt, BLOCK), F32)] * 3
            for h in range(nb):
                hit = high == h
                at = 4 * (h % rb)
                for c in range(3):
                    value[c] = jnp.where(
                        hit, lookup(sums[h // rb, at + c : at + c + 1, :], low), value[c]
                    )
            forces.append([force[3 * a + c] + CHARGE[a] * value[c] for c in range(3)])
        cent = [dense(centres, c) for c in range(3)]
        quat = [quats[c] for c in range(4)]
        torque = [jnp.zeros((wt, BLOCK), F32)] * 3
        for a in range(3):
            lever = [table[3 * a + c] - cent[c] for c in range(3)]
            turn = cross(lever, forces[a])
            torque = [torque[c] + turn[c] for c in range(3)]
        omega = []
        for c in range(3):
            pull = forces[0][c] + forces[1][c] + forces[2][c]
            fast = dense(velocity, c) + STEP_DT * pull / WATER_MASS
            spread(velocity_new, c, fast)
            spread(centres_new, c, cent[c] + STEP_DT * fast)
            spin = dense(angmom, c) + STEP_DT * torque[c]
            spread(angmom_new, c, spin)
            omega.append(spin / INERTIA)
        vector = quat[1:4]
        delta = [-(omega[0] * vector[0] + omega[1] * vector[1] + omega[2] * vector[2])]
        turn = cross(omega, vector)
        delta += [quat[0] * omega[c] + turn[c] for c in range(3)]
        moved = [quat[c] + 0.5 * STEP_DT * delta[c] for c in range(4)]
        length = jnp.sqrt(sum(m * m for m in moved))
        for c in range(4):
            spread(orient_new, c, moved[c] / length)
        pass_on(2)

        def unfold(dr, carry):
            r = lax.rem(row + n_row - dr, n_row)
            arrived(comp.at[r], s_recv.at[dr])
            expand(r)
            return carry

        lax.fori_loop(1, n_row, unfold, 0)
        pass_on(3)
        col_pot = jnp.concatenate(
            [potential[pl.ds(me * cb + j, 1), :] for j in range(cb)], axis=1
        )
        eye = (
            lax.broadcasted_iota(jnp.int32, (BLOCK, BLOCK), 0)
            == lax.broadcasted_iota(jnp.int32, (BLOCK, BLOCK), 1)
        )

        def product(k, _):
            at = pl.ds(pl.multiple_of(k * step, step), step)
            total = jnp.zeros((step, cols), F32)
            for dc in range(n_col):
                for du in range(n_sub):
                    slot = source(dc, du)
                    if du > 0:
                        arrived(panel.at[slot, at], d_recv.at[dc, du, k])
                    depth = pl.ds(pl.multiple_of(slot * cols, cols), cols)
                    total = total + jnp.dot(
                        panel[slot, at, :], full[depth, :], preferred_element_type=F32
                    )
            line = potential[pl.ds(row * rb + k, 1), :]
            row_pot = jnp.sum(jnp.where(eye, line, 0.0), axis=1, keepdims=True)
            mine = panel[me, at, :].astype(F32)
            coupled[at, :] = (total + COUPLE * (row_pot + col_pot) * mine).astype(BF16)
            return 0

        lax.fori_loop(0, CHUNKS, product, 0)

        arrived(hist.at[pl.ds(1, n_all - 1)], h_send)
        arrived(field.at[pl.ds(1, n_all - 1)], q_send)
        pl.when(target != me)(lambda: pass_inner(0).wait_send())
        for dr in range(1, n_row):
            pass_inner(dr).wait_send()
        for copy in started:
            copy.wait_send()

    hbm = pl.BlockSpec(memory_space=pltpu.HBM)
    vmem = pl.BlockSpec(memory_space=pltpu.VMEM)
    dma = lambda *s: pltpu.SemaphoreType.DMA(s)
    one = pltpu.SemaphoreType.DMA(())
    call = pl.pallas_call(
        kernel,
        out_shape=(
            pltpu.VMEM((rows, cols), BF16),
            pltpu.VMEM((3, waters), F32),
            pltpu.VMEM((3, waters), F32),
            pltpu.VMEM((3, waters), F32),
            pltpu.VMEM((4, waters), F32),
        ),
        in_specs=[hbm] * 12,
        out_specs=(vmem,) * 5,
        scratch_shapes=[
            pltpu.VMEM((rows, cols), BF16),
            pltpu.VMEM((rows, cols), BF16),
            pltpu.SMEM((rb, cb), jnp.int32),
            pltpu.SMEM((rb, cb), jnp.int32),
            pltpu.VMEM((3, cols), BF16),
            pltpu.VMEM((3, waters), jnp.int32),
            pltpu.VMEM((3, waters), F32),
            pltpu.VMEM((3, waters), F32),
            pltpu.VMEM((3, waters), F32),
            pltpu.VMEM((3, waters), F32),
            pltpu.VMEM((2, halo), jnp.int32),
            pltpu.VMEM((neigh, waters), jnp.int32),
            pltpu.VMEM((n_m, rows, cols), BF16),
            pltpu.VMEM((n_row, rows + rb * cb, BLOCK), BF16),
            pltpu.VMEM((order, cols), BF16),
            pltpu.VMEM((n_all, nb, BLOCK), jnp.int16),
            pltpu.VMEM((rb * 4, BLOCK), F32),
            pltpu.VMEM((wide, n_m, rb * 4, BLOCK), F32),
            pltpu.VMEM((n_all, rb * 4, BLOCK), BF16),
            pltpu.VMEM((2, 24, BLOCK), F32),
            pltpu.VMEM((2, 24, BLOCK), F32),
            pltpu.VMEM((9, wt, BLOCK), F32),
            pltpu.VMEM((9, wt, BLOCK), F32),
            pltpu.VMEM((4, wt, BLOCK), F32),
            pltpu.VMEM((nb, BLOCK), F32),
            pltpu.VMEM((n_row, rb * 4, BLOCK), F32),
            dma(11), dma(CHUNKS),
            dma(n_col, n_sub, CHUNKS), dma(n_col, n_sub, CHUNKS), dma(n_col, n_sub, CHUNKS),
            dma(n_row), dma(n_row), one, one, dma(n_row), dma(wide, n_m),
            one, one, dma(2), dma(2),
        ],
        compiler_params=pltpu.CompilerParams(
            collective_id=0, has_side_effects=True, vmem_limit_bytes=48 << 20
        ),
    )
    return call


def deliver(results):
    count = len(results)

    def kernel(*refs):
        sem = refs[2 * count]
        stores = [
            pltpu.make_async_copy(refs[n], refs[count + n], sem.at[n]) for n in range(count)
        ]
        for store in stores:
            store.start()
        for store in stores:
            store.wait()

    return pl.pallas_call(
        kernel,
        out_shape=tuple(jax.ShapeDtypeStruct(r.shape, r.dtype) for r in results),
        in_specs=[pl.BlockSpec(memory_space=pltpu.VMEM)] * count,
        out_specs=(pl.BlockSpec(memory_space=pltpu.HBM),) * count,
        scratch_shapes=[pltpu.SemaphoreType.DMA((count,))],
    )(*[pltpu.with_memory_space_constraint(r, pltpu.VMEM) for r in results])


def solution(mesh):
    n_row, n_col, n_sub = mesh.shape["row"], mesh.shape["col"], mesh.shape["sub"]

    def shards(density, margin, pattern_d, pattern_s, dipole, owner, centres, angles,
               velocity, angmom, halo_list, neighbours):
        call = make_kernel(
            n_row, n_col, n_sub, density.shape[0], density.shape[1], owner.shape[1],
            neighbours.shape[0], halo_list.shape[1],
        )
        return deliver(
            call(*[
                pltpu.with_memory_space_constraint(x, pltpu.HBM)
                for x in (density, margin, pattern_d, pattern_s, dipole, owner, centres,
                          angles, velocity, angmom, halo_list, neighbours)
            ])
        )

    block = P(("groups", "row"), ("col", "sub"))
    water = P(None, ("groups", "row", "col", "sub"))
    return jax.shard_map(
        shards,
        mesh=mesh,
        in_specs=(block,) * 4 + (P(None, ("groups", "col", "sub")),) + (water,) * 7,
        out_specs=(block,) + (water,) * 4,
        check_vma=False,
    )
```

time: 34.7 us -> 28.9 us (0.83)
  Pallas kernels: 33.9 us -> 28.1 us
    pallas_call x1, Pallas kernels: 32 us -> 27.2 us  [shards(): call(*[pltpu.with_memory_space_constraint(x, pltpu.HBM) for x in (density...]
    pallas_call x1, Pallas kernels: 1.9 us -> 0.85 us  [deliver(): pl.pallas_call(kernel, out_shape=tuple((jax.ShapeDtypeStruct(r.shape, r.d...]
where the time goes in v1:
time: 28.9 us; the launch traced here: 28.7 us
  Pallas kernels  28.1 us (97%)
  between operations  0.64 us (2%)
    pallas_call x1, Pallas kernels, shards(): call(*[pltpu.with_memory_space_constraint(x, pltpu.HBM) for x in (density...  27.2 us
    pallas_call x1, Pallas kernels, deliver(): pl.pallas_call(kernel, out_shape=tuple((jax.ShapeDtypeStruct(r.shape, r.d...  0.85 us

profile of v1, /device:TPU:0, one launch (start us, length us, event | category | flops | bytes accessed | tf_op | source)
XLA Modules:
  0.0 28.7 jit_solution(8289649291915133768)
XLA Ops:
  0.6 27.2 %shard_map.155 = (bf16[512,512]{1,0:T(8,128)(2,1)S(1)}, f32[3,1024]{1,0:T(4,128)S(1)}, f32[3,1024]{1,0:T(4,128)S(1)}, f32[3,1024]{1,0:T(4,128)S(1)}, f32[4,1024]{1,0:T(4,128)S(1)}) custom-call(bf16[512,512]{1,0:T(8,128)(2,1)} %density_hbm.1, bf16[512,512]{1,0:T(8,128)(2,1)} %margin_hbm.1, s32[4,4]{1,0:T(4,128)} %pat_d_hbm.1, s32[4,4]{1,0:T(4,128)} %pat_s_hbm.1, ...), custom_call_target="tpu_custom_call" | custom-call | tf_op jit(solution)/shard_map/pallas_call | solution.py:569
  27.9 0.8 %shard_map.156 = (bf16[512,512]{1,0:T(8,128)(2,1)}, f32[3,1024]{1,0:T(4,128)}, f32[3,1024]{1,0:T(4,128)}, f32[3,1024]{1,0:T(4,128)}, f32[4,1024]{1,0:T(4,128)}) custom-call(bf16[512,512]{1,0:T(8,128)(2,1)S(1)} %get-tuple-element.10.refs_0_, f32[3,1024]{1,0:T(4,128)S(1)} %get-tuple-element.11.refs_1_, f32[3,1024]{1,0:T(4,128)S(1)} %get-tuple-element.12.refs_2_, ...), custom_call_target="tpu_custom_call" | custom-call | tf_op jit(solution)/shard_map/pallas_call | solution.py:550

commit v2 on v1

--- a/solution.py
+++ b/solution.py
@@ -69,6 +69,7 @@
 def make_kernel(n_row, n_col, n_sub, rows, cols, waters, neigh, halo):
     n_m = n_col * n_sub
     n_all = n_row * n_m
+    n_chip = n_row * n_col
     order = rows * n_row
     rb, cb, nb = rows // BLOCK, cols // BLOCK, order // BLOCK
     wt, nh = waters // BLOCK, halo // BLOCK
@@ -83,9 +84,9 @@
         density, margin, pat_d, pat_s, dipole, owner, centres,
         angles, velocity, angmom, halo_list, neighbours,
         panel, comp, full, hist, inner, parts, field, halo_out, halo_in,
-        table, force, quats, potential, sums,
+        table, force, quats, potential, sums, hist1, field1,
         l_sem, c_sem, d_send, d_recv, f_send, s_send, s_recv, h_send, h_recv, v_send, v_recv,
-        q_send, q_recv, e_send, e_recv,
+        q_send, q_recv, e_send, e_recv, i_send, i_recv, g_send, g_recv,
     ):
         row, col, sub = lax.axis_index("row"), lax.axis_index("col"), lax.axis_index("sub")
         me = col * n_sub + sub
@@ -102,6 +103,12 @@
                 "row": lax.rem(row + dr, n_row),
                 "col": lax.rem(col + lax.div(dm, n_sub), n_col),
                 "sub": lax.rem(sub + lax.rem(dm, n_sub), n_sub),
+            }
+
+        def chip(q):
+            return {
+                "row": lax.rem(row + lax.div(q, n_col), n_row),
+                "col": lax.rem(col + lax.rem(q, n_col), n_col),
             }
 
         def source(dc, du):
@@ -213,7 +220,7 @@
             counts = counts + lax.dot_general(
                 high_hot, low_hot, (((1,), (1,)), ((), ())), preferred_element_type=F32
             )
-        hist[0] = counts.astype(jnp.int32).astype(jnp.int16)
+        hist1[0] = counts.astype(jnp.int32).astype(jnp.int16)
         for load in small[4:8]:
             load.wait()
         cent = [dense(centres, c) for c in range(3)]
@@ -243,11 +250,10 @@
                 halo_out[side, t * nh : (t + 1) * nh, :] = value[side * nh : (side + 1) * nh, :]
         pl.semaphore_wait(barrier, n_all - 1)
 
-        def share(q, carry):
-            remote(hist.at[0], hist.at[q], h_send, h_recv, other(q)).start()
-            return carry
-
-        lax.fori_loop(1, n_all, share, 0)
+        for du in range(1, n_sub):
+            started.append(
+                send(hist1.at[0], hist1.at[du], i_send.at[du], i_recv.at[du], peer(0, du))
+            )
 
         def pass_inner(dr):
             there = peer_row(dr)
@@ -268,19 +274,32 @@
                 send(halo_out.at[side], halo_in.at[side], e_send.at[side], e_recv.at[side],
                      peer_row(by))
             )
-        for k in range(CHUNKS):
+        def send_panel(k):
             at = pl.ds(k * step, step)
             for dc in range(1, n_col):
                 started.append(
                     send(panel.at[me, at], panel.at[me, at], d_send.at[dc, 0, k],
                          d_recv.at[dc, 0, k], peer(dc, 0))
                 )
-            if k == 0:
-                for dr in range(1, n_row):
-                    started.append(
-                        send(comp.at[row], comp.at[row], s_send.at[dr], s_recv.at[dr],
-                             peer_row(dr))
-                    )
+
+        send_panel(0)
+        total = hist1[0].astype(jnp.int32)
+        for du in range(1, n_sub):
+            arrived(hist1.at[du], i_recv.at[du])
+            total = total + hist1[du].astype(jnp.int32)
+        hist[0] = total.astype(jnp.int16)
+
+        def share(q, carry):
+            remote(hist.at[0], hist.at[q], h_send, h_recv, chip(q)).start()
+            return carry
+
+        lax.fori_loop(1, n_chip, share, 0)
+        for dr in range(1, n_row):
+            started.append(
+                send(comp.at[row], comp.at[row], s_send.at[dr], s_recv.at[dr], peer_row(dr))
+            )
+        for k in range(1, CHUNKS):
+            send_panel(k)
         for k in range(CHUNKS):
             at = pl.ds(k * step, step)
             for du in range(1, n_sub):
@@ -342,9 +361,9 @@
             arrived(halo_in.at[side], e_recv.at[side])
         lax.fori_loop(0, wt // 2, pair_tile, 0)
 
-        arrived(hist.at[pl.ds(1, n_all - 1)], h_recv)
+        arrived(hist.at[pl.ds(1, n_chip - 1)], h_recv)
         counts = lax.fori_loop(
-            1, n_all, lambda q, c: c + hist[q].astype(jnp.int32), hist[0].astype(jnp.int32)
+            1, n_chip, lambda q, c: c + hist[q].astype(jnp.int32), hist[0].astype(jnp.int32)
         )
         potential[...] = counts.astype(F32) * UNIT
         for s in range(wide):
@@ -377,24 +396,71 @@
             weigh = COUPLE * potential[pl.ds(row * rb + i, 1), :]
             inner2 = got[0:3, :] + got[3:6, :] + weigh * got[6:9, :]
             low_u[i] = jnp.concatenate([inner2, jnp.zeros((1, BLOCK), F32)], axis=0)
-        field[0] = jnp.concatenate(low_u, axis=0).astype(BF16)
+        local = jnp.concatenate(low_u, axis=0)
+        field1[0] = local
+        for du in range(1, n_sub):
+            started.append(
+                send(field1.at[0], field1.at[du], g_send.at[du], g_recv.at[du], peer(0, du))
+            )
+        for du in range(1, n_sub):
+            arrived(field1.at[du], g_recv.at[du])
+            local = local + field1[du]
+        field[0] = local.astype(BF16)
 
         def tell(q, carry):
-            remote(field.at[0], field.at[q], q_send, q_recv, other(q)).start()
+            remote(field.at[0], field.at[q], q_send, q_recv, chip(q)).start()
             return carry
 
-        lax.fori_loop(1, n_all, tell, 0)
+        lax.fori_loop(1, n_chip, tell, 0)
         pass_on(0)
         lax.fori_loop(wt // 2, wt, pair_tile, 0)
         pass_on(1)
 
-        arrived(field.at[pl.ds(1, n_all - 1)], q_recv)
+        pass_on(2)
+
+        def unfold(dr, carry):
+            r = lax.rem(row + n_row - dr, n_row)
+            arrived(comp.at[r], s_recv.at[dr])
+            expand(r)
+            return carry
+
+        lax.fori_loop(1, n_row, unfold, 0)
+        pass_on(3)
+        col_pot = jnp.concatenate(
+            [potential[pl.ds(me * cb + j, 1), :] for j in range(cb)], axis=1
+        )
+        eye = (
+            lax.broadcasted_iota(jnp.int32, (BLOCK, BLOCK), 0)
+            == lax.broadcasted_iota(jnp.int32, (BLOCK, BLOCK), 1)
+        )
+
+        def product(k, _):
+            at = pl.ds(pl.multiple_of(k * step, step), step)
+            total = jnp.zeros((step, cols), F32)
+            for dc in range(n_col):
+                for du in range(n_sub):
+                    slot = source(dc, du)
+                    if du > 0:
+                        arrived(panel.at[slot, at], d_recv.at[dc, du, k])
+                    depth = pl.ds(pl.multiple_of(slot * cols, cols), cols)
+                    total = total + jnp.dot(
+                        panel[slot, at, :], full[depth, :], preferred_element_type=F32
+                    )
+            line = potential[pl.ds(row * rb + k, 1), :]
+            row_pot = jnp.sum(jnp.where(eye, line, 0.0), axis=1, keepdims=True)
+            mine = panel[me, at, :].astype(F32)
+            coupled[at, :] = (total + COUPLE * (row_pot + col_pot) * mine).astype(BF16)
+            return 0
+
+        lax.fori_loop(0, CHUNKS, product, 0)
+
+        arrived(field.at[pl.ds(1, n_chip - 1)], q_recv)
         small[8].wait()
         small[9].wait()
         for dr in range(n_row):
-            total = field[dr * n_m].astype(F32)
-            for m in range(1, n_m):
-                total = total + field[dr * n_m + m].astype(F32)
+            total = field[dr * n_col].astype(F32)
+            for m in range(1, n_col):
+                total = total + field[dr * n_col + m].astype(F32)
             sums[lax.rem(row + n_row - dr, n_row)] = total
 
         forces = []
@@ -434,46 +500,9 @@
         length = jnp.sqrt(sum(m * m for m in moved))
         for c in range(4):
             spread(orient_new, c, moved[c] / length)
-        pass_on(2)
-
-        def unfold(dr, carry):
-            r = lax.rem(row + n_row - dr, n_row)
-            arrived(comp.at[r], s_recv.at[dr])
-            expand(r)
-            return carry
-
-        lax.fori_loop(1, n_row, unfold, 0)
-        pass_on(3)
-        col_pot = jnp.concatenate(
-            [potential[pl.ds(me * cb + j, 1), :] for j in range(cb)], axis=1
-        )
-        eye = (
-            lax.broadcasted_iota(jnp.int32, (BLOCK, BLOCK), 0)
-            == lax.broadcasted_iota(jnp.int32, (BLOCK, BLOCK), 1)
-        )
-
-        def product(k, _):
-            at = pl.ds(pl.multiple_of(k * step, step), step)
-            total = jnp.zeros((step, cols), F32)
-            for dc in range(n_col):
-                for du in range(n_sub):
-                    slot = source(dc, du)
-                    if du > 0:
-                        arrived(panel.at[slot, at], d_recv.at[dc, du, k])
-                    depth = pl.ds(pl.multiple_of(slot * cols, cols), cols)
-                    total = total + jnp.dot(
-                        panel[slot, at, :], full[depth, :], preferred_element_type=F32
-                    )
-            line = potential[pl.ds(row * rb + k, 1), :]
-            row_pot = jnp.sum(jnp.where(eye, line, 0.0), axis=1, keepdims=True)
-            mine = panel[me, at, :].astype(F32)
-            coupled[at, :] = (total + COUPLE * (row_pot + col_pot) * mine).astype(BF16)
-            return 0
-
-        lax.fori_loop(0, CHUNKS, product, 0)
-
-        arrived(hist.at[pl.ds(1, n_all - 1)], h_send)
-        arrived(field.at[pl.ds(1, n_all - 1)], q_send)
+
+        arrived(hist.at[pl.ds(1, n_chip - 1)], h_send)
+        arrived(field.at[pl.ds(1, n_chip - 1)], q_send)
         pl.when(target != me)(lambda: pass_inner(0).wait_send())
         for dr in range(1, n_row):
             pass_inner(dr).wait_send()
@@ -511,10 +540,10 @@
             pltpu.VMEM((n_m, rows, cols), BF16),
             pltpu.VMEM((n_row, rows + rb * cb, BLOCK), BF16),
             pltpu.VMEM((order, cols), BF16),
-            pltpu.VMEM((n_all, nb, BLOCK), jnp.int16),
+            pltpu.VMEM((n_chip, nb, BLOCK), jnp.int16),
             pltpu.VMEM((rb * 4, BLOCK), F32),
             pltpu.VMEM((wide, n_m, rb * 4, BLOCK), F32),
-            pltpu.VMEM((n_all, rb * 4, BLOCK), BF16),
+            pltpu.VMEM((n_chip, rb * 4, BLOCK), BF16),
             pltpu.VMEM((2, 24, BLOCK), F32),
             pltpu.VMEM((2, 24, BLOCK), F32),
             pltpu.VMEM((9, wt, BLOCK), F32),
@@ -522,10 +551,12 @@
             pltpu.VMEM((4, wt, BLOCK), F32),
             pltpu.VMEM((nb, BLOCK), F32),
             pltpu.VMEM((n_row, rb * 4, BLOCK), F32),
+            pltpu.VMEM((n_sub, nb, BLOCK), jnp.int16),
+            pltpu.VMEM((n_sub, rb * 4, BLOCK), F32),
             dma(11), dma(CHUNKS),
             dma(n_col, n_sub, CHUNKS), dma(n_col, n_sub, CHUNKS), dma(n_col, n_sub, CHUNKS),
             dma(n_row), dma(n_row), one, one, dma(n_row), dma(wide, n_m),
-            one, one, dma(2), dma(2),
+            one, one, dma(2), dma(2), dma(n_sub), dma(n_sub), dma(n_sub), dma(n_sub),
         ],
         compiler_params=pltpu.CompilerParams(
             collective_id=0, has_side_effects=True, vmem_limit_bytes=48 << 20

time: 28.9 us -> 25.5 us (0.88)
  Pallas kernels: 28.1 us -> 24.7 us
    pallas_call x1, Pallas kernels: 27.2 us -> 23.9 us  [shards(): call(*[pltpu.with_memory_space_constraint(x, pltpu.HBM) for x in (density...]
where the time goes in v2:
time: 25.5 us; the launch traced here: 25.4 us
  Pallas kernels  24.7 us (97%)
  between operations  0.64 us (3%)
    pallas_call x1, Pallas kernels, shards(): call(*[pltpu.with_memory_space_constraint(x, pltpu.HBM) for x in (density...  23.9 us
    pallas_call x1, Pallas kernels, deliver(): pl.pallas_call(kernel, out_shape=tuple((jax.ShapeDtypeStruct(r.shape, r.d...  0.85 us

profile of v2, /device:TPU:0, one launch (start us, length us, event | category | flops | bytes accessed | tf_op | source)
XLA Modules:
  0.0 25.4 jit_solution(11876489155117239558)
XLA Ops:
  0.6 23.9 %shard_map.155 = (bf16[512,512]{1,0:T(8,128)(2,1)S(1)}, f32[3,1024]{1,0:T(4,128)S(1)}, f32[3,1024]{1,0:T(4,128)S(1)}, f32[3,1024]{1,0:T(4,128)S(1)}, f32[4,1024]{1,0:T(4,128)S(1)}) custom-call(bf16[512,512]{1,0:T(8,128)(2,1)} %density_hbm.1, bf16[512,512]{1,0:T(8,128)(2,1)} %margin_hbm.1, s32[4,4]{1,0:T(4,128)} %pat_d_hbm.1, s32[4,4]{1,0:T(4,128)} %pat_s_hbm.1, ...), custom_call_target="tpu_custom_call" | custom-call | tf_op jit(solution)/shard_map/pallas_call | solution.py:600
  24.5 0.8 %shard_map.156 = (bf16[512,512]{1,0:T(8,128)(2,1)}, f32[3,1024]{1,0:T(4,128)}, f32[3,1024]{1,0:T(4,128)}, f32[3,1024]{1,0:T(4,128)}, f32[4,1024]{1,0:T(4,128)}) custom-call(bf16[512,512]{1,0:T(8,128)(2,1)S(1)} %get-tuple-element.10.refs_0_, f32[3,1024]{1,0:T(4,128)S(1)} %get-tuple-element.11.refs_1_, f32[3,1024]{1,0:T(4,128)S(1)} %get-tuple-element.12.refs_2_, ...), custom_call_target="tpu_custom_call" | custom-call | tf_op jit(solution)/shard_map/pallas_call | solution.py:581

commit v3 on v2

--- a/solution.py
+++ b/solution.py
@@ -16,6 +16,7 @@
 INERTIA = 0.5
 SOFTEN = 1.0
 CHUNKS = 4
+SPLIT = 2
 F32 = jnp.float32
 BF16 = jnp.bfloat16
 
@@ -83,10 +84,10 @@
         coupled, centres_new, velocity_new, angmom_new, orient_new,
         density, margin, pat_d, pat_s, dipole, owner, centres,
         angles, velocity, angmom, halo_list, neighbours,
-        panel, comp, full, hist, inner, parts, field, halo_out, halo_in,
+        panel, comp, full, total_out, picked, hist, inner, parts, field, halo_out, halo_in,
         table, force, quats, potential, sums, hist1, field1,
         l_sem, c_sem, d_send, d_recv, f_send, s_send, s_recv, h_send, h_recv, v_send, v_recv,
-        q_send, q_recv, e_send, e_recv, i_send, i_recv, g_send, g_recv,
+        q_send, q_recv, e_send, e_recv, row_ready, all_ready, i_send, i_recv, g_send, g_recv,
     ):
         row, col, sub = lax.axis_index("row"), lax.axis_index("col"), lax.axis_index("sub")
         me = col * n_sub + sub
@@ -134,11 +135,47 @@
 
         barrier = pltpu.get_barrier_semaphore()
 
-        def greet(q, carry):
+        def greet(dev):
             pl.semaphore_signal(
-                barrier, inc=1, device_id=other(q), device_id_type=pl.DeviceIdType.MESH
-            )
+                barrier, inc=1, device_id=dev, device_id_type=pl.DeviceIdType.MESH
+            )
+
+        near, far = 0, n_sub - 1
+
+        def greet_near(q, carry):
+            greet({"col": lax.rem(col + q, n_col), "sub": near})
             return carry
+
+        def greet_far(q, carry):
+            greet({
+                "row": lax.rem(row + lax.div(q, n_col), n_row),
+                "col": lax.rem(col + lax.rem(q, n_col), n_col), "sub": far,
+            })
+            return carry
+
+        def in_row():
+            @pl.when(sub == near)
+            def _():
+                pl.semaphore_wait(barrier, n_m - 1)
+                for du in range(1, n_sub):
+                    pl.semaphore_signal(
+                        row_ready, inc=1, device_id=peer(0, du),
+                        device_id_type=pl.DeviceIdType.MESH,
+                    )
+
+            pl.when(sub != near)(lambda: pl.semaphore_wait(row_ready, 1))
+
+        def in_all():
+            @pl.when(sub == far)
+            def _():
+                pl.semaphore_wait(barrier, n_all - n_m)
+                for du in range(1, n_sub):
+                    pl.semaphore_signal(
+                        all_ready, inc=1, device_id=peer(0, du),
+                        device_id_type=pl.DeviceIdType.MESH,
+                    )
+
+            pl.when(sub != far)(lambda: pl.semaphore_wait(all_ready, 1))
 
         small = [
             pltpu.make_async_copy(src, dst, l_sem.at[n])
@@ -163,7 +200,9 @@
         small[10].start()
         for load in small[1:10]:
             load.start()
-        lax.fori_loop(1, n_all, greet, 0)
+        lax.fori_loop(1, n_col, greet_near, 0)
+        pl.when(sub != near)(lambda: greet({"sub": near}))
+        lax.fori_loop(n_col, n_chip, greet_far, 0)
 
         small[0].wait()
         for k in range(CHUNKS):
@@ -174,6 +213,29 @@
                     ac = slice(j * BLOCK, (j + 1) * BLOCK)
                     factor = pat_d[i, j].astype(F32)
                     panel[me, at, ac] = (density[at, ac].astype(F32) * factor).astype(BF16)
+        in_row()
+        def panel_copy(dc, k):
+            at = panel.at[me, pl.ds(k * step, step)]
+            return remote(at, at, d_send.at[dc, 0, k], d_recv.at[dc, 0, k], peer(dc, 0))
+
+        rank = jnp.minimum(row, 2)
+
+        def send_panels(first, end):
+            for k in range(CHUNKS):
+                @pl.when(jnp.logical_and(k + rank >= first, k + rank < end))
+                def _(k=k):
+                    for dc in range(1, n_col):
+                        panel_copy(dc, k).start()
+
+        send_panels(0, 2)
+        for k in range(CHUNKS):
+            at = pl.ds(k * step, step)
+            for du in range(1, n_sub):
+                started.append(
+                    send(panel.at[me, at], panel.at[me, at], d_send.at[0, du, k],
+                         d_recv.at[0, du, k], peer(0, du))
+                )
+
         small[1].wait()
         small[2].wait()
         small[10].wait()
@@ -221,6 +283,11 @@
                 high_hot, low_hot, (((1,), (1,)), ((), ())), preferred_element_type=F32
             )
         hist1[0] = counts.astype(jnp.int32).astype(jnp.int16)
+        for du in range(1, n_sub):
+            started.append(
+                send(hist1.at[0], hist1.at[du], i_send.at[du], i_recv.at[du], peer(0, du))
+            )
+
         for load in small[4:8]:
             load.wait()
         cent = [dense(centres, c) for c in range(3)]
@@ -248,12 +315,7 @@
                 value = jnp.where(high == h, lookup(table[t, h : h + 1, :], low), value)
             for side in range(2):
                 halo_out[side, t * nh : (t + 1) * nh, :] = value[side * nh : (side + 1) * nh, :]
-        pl.semaphore_wait(barrier, n_all - 1)
-
-        for du in range(1, n_sub):
-            started.append(
-                send(hist1.at[0], hist1.at[du], i_send.at[du], i_recv.at[du], peer(0, du))
-            )
+        in_all()
 
         def pass_inner(dr):
             there = peer_row(dr)
@@ -274,15 +336,6 @@
                 send(halo_out.at[side], halo_in.at[side], e_send.at[side], e_recv.at[side],
                      peer_row(by))
             )
-        def send_panel(k):
-            at = pl.ds(k * step, step)
-            for dc in range(1, n_col):
-                started.append(
-                    send(panel.at[me, at], panel.at[me, at], d_send.at[dc, 0, k],
-                         d_recv.at[dc, 0, k], peer(dc, 0))
-                )
-
-        send_panel(0)
         total = hist1[0].astype(jnp.int32)
         for du in range(1, n_sub):
             arrived(hist1.at[du], i_recv.at[du])
@@ -294,25 +347,28 @@
             return carry
 
         lax.fori_loop(1, n_chip, share, 0)
-        for dr in range(1, n_row):
-            started.append(
-                send(comp.at[row], comp.at[row], s_send.at[dr], s_recv.at[dr], peer_row(dr))
-            )
-        for k in range(1, CHUNKS):
-            send_panel(k)
-        for k in range(CHUNKS):
-            at = pl.ds(k * step, step)
-            for du in range(1, n_sub):
-                started.append(
-                    send(panel.at[me, at], panel.at[me, at], d_send.at[0, du, k],
-                         d_recv.at[0, du, k], peer(0, du))
-                )
-
+
+        def pass_block(to):
+            return remote(
+                comp.at[row], comp.at[row], s_send.at[to], s_recv.at[row], {"row": to}
+            )
+
+        upper = lax.div(row, n_row // 2)
+        inner_row = n_row // 2 - upper
+
+        def pass_blocks(early):
+            for to in range(n_row):
+                held = to == inner_row
+                go = jnp.logical_not(held) if early else held
+                pl.when(jnp.logical_and(row != to, go))(lambda to=to: pass_block(to).start())
+
+        pass_blocks(True)
+        send_panels(2, 6)
         def expand(r):
             marks = comp[r, rows : rows + rb * cb, :].astype(F32)
             for i in range(rb):
                 tile = comp[r, i * BLOCK : (i + 1) * BLOCK, :].astype(F32)
-                at = pl.ds(pl.multiple_of(r * rows + i * BLOCK, BLOCK), BLOCK)
+                at = slice(i * BLOCK, (i + 1) * BLOCK)
                 for j in range(cb):
                     q = i * cb + j
                     full[at, j * BLOCK : (j + 1) * BLOCK] = (tile * marks[q : q + 1, :]).astype(BF16)
@@ -328,22 +384,33 @@
                              d_recv.at[dc, du, k], peer(0, du))
                     )
 
+        def pick_own(j, carry):
+            lanes = pl.ds(pl.multiple_of(j * BLOCK, BLOCK), BLOCK)
+            for s in range(neigh // 8):
+                idx = neighbours[8 * s : 8 * s + 8, lanes]
+                low, high = idx & (BLOCK - 1), idx >> 7
+                part = [lookup(table[t, 0:1, :], low) for t in range(9)]
+                for h in range(1, wt):
+                    hit = high == h
+                    for t in range(9):
+                        part[t] = jnp.where(hit, lookup(table[t, h : h + 1, :], low), part[t])
+                for t in range(9):
+                    picked[j, s, t] = part[t]
+            return carry
+
         def pair_tile(j, carry):
             lanes = pl.ds(pl.multiple_of(j * BLOCK, BLOCK), BLOCK)
             own = [jnp.broadcast_to(table[t, pl.ds(j, 1), :], (8, BLOCK)) for t in range(9)]
             totals = [jnp.zeros((8, BLOCK), F32) for _ in range(9)]
-            for s in range(0, neigh, 8):
-                idx = neighbours[s : s + 8, lanes]
+            for s in range(neigh // 8):
+                idx = neighbours[8 * s : 8 * s + 8, lanes]
                 low, high = idx & (BLOCK - 1), idx >> 7
-                part = [lookup(table[t, 0:1, :], low) for t in range(9)]
-                for h in range(1, wt + 2 * nh):
+                part = [picked[j, s, t] for t in range(9)]
+                for h in range(wt, wt + 2 * nh):
                     hit = high == h
+                    side, at = (h - wt) // nh, (h - wt) % nh
                     for t in range(9):
-                        if h < wt:
-                            line = table[t, h : h + 1, :]
-                        else:
-                            side, at = (h - wt) // nh, t * nh + (h - wt) % nh
-                            line = halo_in[side, at : at + 1, :]
+                        line = halo_in[side, t * nh + at : t * nh + at + 1, :]
                         part[t] = jnp.where(hit, lookup(line, low), part[t])
                 for a in range(3):
                     for b in range(3):
@@ -356,10 +423,7 @@
                 force[t, pl.ds(j, 1), :] = jnp.sum(totals[t], axis=0, keepdims=True)
             return carry
 
-        expand(row)
-        for side in range(2):
-            arrived(halo_in.at[side], e_recv.at[side])
-        lax.fori_loop(0, wt // 2, pair_tile, 0)
+        lax.fori_loop(0, wt, pick_own, 0)
 
         arrived(hist.at[pl.ds(1, n_chip - 1)], h_recv)
         counts = lax.fori_loop(
@@ -402,6 +466,9 @@
             started.append(
                 send(field1.at[0], field1.at[du], g_send.at[du], g_recv.at[du], peer(0, du))
             )
+        for side in range(2):
+            arrived(halo_in.at[side], e_recv.at[side])
+        lax.fori_loop(0, wt // 4, pair_tile, 0)
         for du in range(1, n_sub):
             arrived(field1.at[du], g_recv.at[du])
             local = local + field1[du]
@@ -412,20 +479,12 @@
             return carry
 
         lax.fori_loop(1, n_chip, tell, 0)
+        pass_blocks(False)
+        send_panels(6, CHUNKS + 2)
         pass_on(0)
-        lax.fori_loop(wt // 2, wt, pair_tile, 0)
+        lax.fori_loop(wt // 4, wt, pair_tile, 0)
         pass_on(1)
 
-        pass_on(2)
-
-        def unfold(dr, carry):
-            r = lax.rem(row + n_row - dr, n_row)
-            arrived(comp.at[r], s_recv.at[dr])
-            expand(r)
-            return carry
-
-        lax.fori_loop(1, n_row, unfold, 0)
-        pass_on(3)
         col_pot = jnp.concatenate(
             [potential[pl.ds(me * cb + j, 1), :] for j in range(cb)], axis=1
         )
@@ -434,25 +493,49 @@
             == lax.broadcasted_iota(jnp.int32, (BLOCK, BLOCK), 1)
         )
 
-        def product(k, _):
-            at = pl.ds(pl.multiple_of(k * step, step), step)
-            total = jnp.zeros((step, cols), F32)
-            for dc in range(n_col):
-                for du in range(n_sub):
-                    slot = source(dc, du)
-                    if du > 0:
-                        arrived(panel.at[slot, at], d_recv.at[dc, du, k])
-                    depth = pl.ds(pl.multiple_of(slot * cols, cols), cols)
-                    total = total + jnp.dot(
-                        panel[slot, at, :], full[depth, :], preferred_element_type=F32
-                    )
+        def term(r, at):
+            depth = pl.ds(pl.multiple_of(lax.rem(r, wide) * rows, rows), rows)
+            return jnp.dot(
+                panel[lax.div(r, wide), at, depth], full[...], preferred_element_type=F32
+            )
+
+        def source_row(t):
+            return t - 1 + lax.div(t - 1 + n_row - row, n_row)
+
+        def block(r):
+            arrived(comp.at[r], s_recv.at[r])
+            expand(r)
+
+        pass_on(2)
+        pass_on(3)
+        for dc in range(n_col):
+            for du in range(1, n_sub):
+                for k in range(CHUNKS):
+                    at = pl.ds(k * step, step)
+                    arrived(panel.at[source(dc, du), at], d_recv.at[dc, du, k])
+        parts_of = [slice(k * rows // SPLIT, (k + 1) * rows // SPLIT) for k in range(SPLIT)]
+        expand(row)
+        for at in parts_of:
+            total_out[at, :] = term(row, at)
+
+        def add_block(t, carry):
+            r = source_row(t)
+            block(r)
+            for at in parts_of:
+                total_out[at, :] += term(r, at)
+            return carry
+
+        lax.fori_loop(1, n_row - 1, add_block, 0)
+        last = source_row(n_row - 1)
+        block(last)
+        for k in range(rb):
+            at = slice(k * BLOCK, (k + 1) * BLOCK)
             line = potential[pl.ds(row * rb + k, 1), :]
             row_pot = jnp.sum(jnp.where(eye, line, 0.0), axis=1, keepdims=True)
             mine = panel[me, at, :].astype(F32)
-            coupled[at, :] = (total + COUPLE * (row_pot + col_pot) * mine).astype(BF16)
-            return 0
-
-        lax.fori_loop(0, CHUNKS, product, 0)
+            coupled[at, :] = (
+                total_out[at, :] + term(last, at) + COUPLE * (row_pot + col_pot) * mine
+            ).astype(BF16)
 
         arrived(field.at[pl.ds(1, n_chip - 1)], q_recv)
         small[8].wait()
@@ -506,6 +589,11 @@
         pl.when(target != me)(lambda: pass_inner(0).wait_send())
         for dr in range(1, n_row):
             pass_inner(dr).wait_send()
+        for to in range(n_row):
+            pl.when(row != to)(lambda to=to: pass_block(to).wait_send())
+        for dc in range(1, n_col):
+            for k in range(CHUNKS):
+                panel_copy(dc, k).wait_send()
         for copy in started:
             copy.wait_send()
 
@@ -539,7 +627,9 @@
             pltpu.VMEM((neigh, waters), jnp.int32),
             pltpu.VMEM((n_m, rows, cols), BF16),
             pltpu.VMEM((n_row, rows + rb * cb, BLOCK), BF16),
-            pltpu.VMEM((order, cols), BF16),
+            pltpu.VMEM((rows, cols), BF16),
+            pltpu.VMEM((rows, cols), F32),
+            pltpu.VMEM((wt, neigh // 8, 9, 8, BLOCK), F32),
             pltpu.VMEM((n_chip, nb, BLOCK), jnp.int16),
             pltpu.VMEM((rb * 4, BLOCK), F32),
             pltpu.VMEM((wide, n_m, rb * 4, BLOCK), F32),
@@ -556,7 +646,8 @@
             dma(11), dma(CHUNKS),
             dma(n_col, n_sub, CHUNKS), dma(n_col, n_sub, CHUNKS), dma(n_col, n_sub, CHUNKS),
             dma(n_row), dma(n_row), one, one, dma(n_row), dma(wide, n_m),
-            one, one, dma(2), dma(2), dma(n_sub), dma(n_sub), dma(n_sub), dma(n_sub),
+            one, one, dma(2), dma(2), pltpu.SemaphoreType.REGULAR, pltpu.SemaphoreType.REGULAR,
+            dma(n_sub), dma(n_sub), dma(n_sub), dma(n_sub),
         ],
         compiler_params=pltpu.CompilerParams(
             collective_id=0, has_side_effects=True, vmem_limit_bytes=48 << 20

time: 25.5 us -> 24.2 us (0.949)
  the two profiles are of different devices: /device:TPU:0 before, /device:TPU:25 now
where the time goes in v3:
time: 24.2 us; the launch traced here: 24.1 us
  Pallas kernels  23.4 us (97%)
  between operations  0.64 us (3%)
    pallas_call x1, Pallas kernels, shards(): call(*[pltpu.with_memory_space_constraint(x, pltpu.HBM) for x in (density...  22.6 us
    pallas_call x1, Pallas kernels, deliver(): pl.pallas_call(kernel, out_shape=tuple((jax.ShapeDtypeStruct(r.shape, r.d...  0.85 us

profile of v3, /device:TPU:25, one launch (start us, length us, event | category | flops | bytes accessed | tf_op | source)
XLA Modules:
  0.0 24.1 jit_solution(1162804060995319641)
XLA Ops:
  0.6 22.6 %shard_map.155 = (bf16[512,512]{1,0:T(8,128)(2,1)S(1)}, f32[3,1024]{1,0:T(4,128)S(1)}, f32[3,1024]{1,0:T(4,128)S(1)}, f32[3,1024]{1,0:T(4,128)S(1)}, f32[4,1024]{1,0:T(4,128)S(1)}) custom-call(bf16[512,512]{1,0:T(8,128)(2,1)} %density_hbm.1, bf16[512,512]{1,0:T(8,128)(2,1)} %margin_hbm.1, s32[4,4]{1,0:T(4,128)} %pat_d_hbm.1, s32[4,4]{1,0:T(4,128)} %pat_s_hbm.1, ...), custom_call_target="tpu_custom_call" | custom-call | tf_op jit(solution)/shard_map/pallas_call | solution.py:691
  23.2 0.8 %shard_map.156 = (bf16[512,512]{1,0:T(8,128)(2,1)}, f32[3,1024]{1,0:T(4,128)}, f32[3,1024]{1,0:T(4,128)}, f32[3,1024]{1,0:T(4,128)}, f32[4,1024]{1,0:T(4,128)}) custom-call(bf16[512,512]{1,0:T(8,128)(2,1)S(1)} %get-tuple-element.10.refs_0_, f32[3,1024]{1,0:T(4,128)S(1)} %get-tuple-element.11.refs_1_, f32[3,1024]{1,0:T(4,128)S(1)} %get-tuple-element.12.refs_2_, ...), custom_call_target="tpu_custom_call" | custom-call | tf_op jit(solution)/shard_map/pallas_call | solution.py:672

commit v4 on v3

--- a/solution.py
+++ b/solution.py
@@ -193,16 +193,35 @@
             )
             for k in range(CHUNKS)
         ]
+        small[3].start()
         small[0].start()
         loads[0].start()
         for load in loads[1:]:
             load.start()
         small[10].start()
-        for load in small[1:10]:
-            load.start()
+        for n in (1, 2, 4, 5, 6, 7, 8, 9):
+            small[n].start()
         lax.fori_loop(1, n_col, greet_near, 0)
         pl.when(sub != near)(lambda: greet({"sub": near}))
         lax.fori_loop(n_col, n_chip, greet_far, 0)
+
+        small[3].wait()
+        lane_ids = lax.broadcasted_iota(jnp.int32, (BLOCK, waters), 0)
+        high_ids = lax.broadcasted_iota(jnp.int32, (nb, waters), 0)
+        counts = jnp.zeros((nb, BLOCK), F32)
+        for site in range(3):
+            own = owner[site : site + 1, :]
+            low_hot = jnp.where(lane_ids == (own & (BLOCK - 1)), 1.0, 0.0).astype(BF16)
+            high_hot = jnp.where(high_ids == (own >> 7), WEIGHT[site], 0.0).astype(BF16)
+            counts = counts + lax.dot_general(
+                high_hot, low_hot, (((1,), (1,)), ((), ())), preferred_element_type=F32
+            )
+        hist1[0] = counts.astype(jnp.int32).astype(jnp.int16)
+        in_row()
+        for du in range(1, n_sub):
+            started.append(
+                send(hist1.at[0], hist1.at[du], i_send.at[du], i_recv.at[du], peer(0, du))
+            )
 
         small[0].wait()
         for k in range(CHUNKS):
@@ -213,7 +232,6 @@
                     ac = slice(j * BLOCK, (j + 1) * BLOCK)
                     factor = pat_d[i, j].astype(F32)
                     panel[me, at, ac] = (density[at, ac].astype(F32) * factor).astype(BF16)
-        in_row()
         def panel_copy(dc, k):
             at = panel.at[me, pl.ds(k * step, step)]
             return remote(at, at, d_send.at[dc, 0, k], d_recv.at[dc, 0, k], peer(dc, 0))
@@ -270,23 +288,6 @@
         for i in range(rb):
             inner[4 * i : 4 * i + 3, :] = low_u[i]
             inner[4 * i + 3 : 4 * i + 4, :] = low_u[i][0:1, :]
-
-        small[3].wait()
-        lane_ids = lax.broadcasted_iota(jnp.int32, (BLOCK, waters), 0)
-        high_ids = lax.broadcasted_iota(jnp.int32, (nb, waters), 0)
-        counts = jnp.zeros((nb, BLOCK), F32)
-        for site in range(3):
-            own = owner[site : site + 1, :]
-            low_hot = jnp.where(lane_ids == (own & (BLOCK - 1)), 1.0, 0.0).astype(BF16)
-            high_hot = jnp.where(high_ids == (own >> 7), WEIGHT[site], 0.0).astype(BF16)
-            counts = counts + lax.dot_general(
-                high_hot, low_hot, (((1,), (1,)), ((), ())), preferred_element_type=F32
-            )
-        hist1[0] = counts.astype(jnp.int32).astype(jnp.int16)
-        for du in range(1, n_sub):
-            started.append(
-                send(hist1.at[0], hist1.at[du], i_send.at[du], i_recv.at[du], peer(0, du))
-            )
 
         for load in small[4:8]:
             load.wait()
@@ -354,7 +355,7 @@
             )
 
         upper = lax.div(row, n_row // 2)
-        inner_row = n_row // 2 - upper
+        inner_row = n_row - 1 - upper * (n_row // 2)
 
         def pass_blocks(early):
             for to in range(n_row):
@@ -371,7 +372,7 @@
                 at = slice(i * BLOCK, (i + 1) * BLOCK)
                 for j in range(cb):
                     q = i * cb + j
-                    full[at, j * BLOCK : (j + 1) * BLOCK] = (tile * marks[q : q + 1, :]).astype(BF16)
+                    full[r, at, j * BLOCK : (j + 1) * BLOCK] = (tile * marks[q : q + 1, :]).astype(BF16)
 
         def pass_on(k):
             at = pl.ds(k * step, step)
@@ -493,50 +494,23 @@
             == lax.broadcasted_iota(jnp.int32, (BLOCK, BLOCK), 1)
         )
 
-        def term(r, at):
-            depth = pl.ds(pl.multiple_of(lax.rem(r, wide) * rows, rows), rows)
-            return jnp.dot(
-                panel[lax.div(r, wide), at, depth], full[...], preferred_element_type=F32
-            )
-
-        def source_row(t):
-            return t - 1 + lax.div(t - 1 + n_row - row, n_row)
-
-        def block(r):
-            arrived(comp.at[r], s_recv.at[r])
-            expand(r)
+        def term(slot, at):
+            total = None
+            for s in range(wide):
+                part = jnp.dot(
+                    panel[slot, at, s * rows : (s + 1) * rows], full[slot * wide + s],
+                    preferred_element_type=F32,
+                )
+                total = part if total is None else total + part
+            return total
+
+        def blocks(slot):
+            for s in range(wide):
+                r = slot * wide + s
+                pl.when(r != row)(lambda r=r: arrived(comp.at[r], s_recv.at[r]))
+                expand(r)
 
         pass_on(2)
-        pass_on(3)
-        for dc in range(n_col):
-            for du in range(1, n_sub):
-                for k in range(CHUNKS):
-                    at = pl.ds(k * step, step)
-                    arrived(panel.at[source(dc, du), at], d_recv.at[dc, du, k])
-        parts_of = [slice(k * rows // SPLIT, (k + 1) * rows // SPLIT) for k in range(SPLIT)]
-        expand(row)
-        for at in parts_of:
-            total_out[at, :] = term(row, at)
-
-        def add_block(t, carry):
-            r = source_row(t)
-            block(r)
-            for at in parts_of:
-                total_out[at, :] += term(r, at)
-            return carry
-
-        lax.fori_loop(1, n_row - 1, add_block, 0)
-        last = source_row(n_row - 1)
-        block(last)
-        for k in range(rb):
-            at = slice(k * BLOCK, (k + 1) * BLOCK)
-            line = potential[pl.ds(row * rb + k, 1), :]
-            row_pot = jnp.sum(jnp.where(eye, line, 0.0), axis=1, keepdims=True)
-            mine = panel[me, at, :].astype(F32)
-            coupled[at, :] = (
-                total_out[at, :] + term(last, at) + COUPLE * (row_pot + col_pot) * mine
-            ).astype(BF16)
-
         arrived(field.at[pl.ds(1, n_chip - 1)], q_recv)
         small[8].wait()
         small[9].wait()
@@ -584,6 +558,38 @@
         for c in range(4):
             spread(orient_new, c, moved[c] / length)
 
+        pass_on(3)
+        flip = lax.rem(upper + lax.div(col, n_col // 2), 2)
+        for p in range(n_col - 1):
+            dc = lax.rem(p + flip, n_col)
+            for du in range(n_sub):
+                slot = source(dc, du)
+                if du > 0:
+                    for k in range(CHUNKS):
+                        arrived(panel.at[slot, pl.ds(k * step, step)], d_recv.at[dc, du, k])
+                blocks(slot)
+                for q in range(SPLIT):
+                    at = slice(q * rows // SPLIT, (q + 1) * rows // SPLIT)
+                    if p + du == 0:
+                        total_out[at, :] = term(slot, at)
+                    else:
+                        total_out[at, :] += term(slot, at)
+        dc = lax.rem(n_col - 1 + flip, n_col)
+        for du in range(n_sub):
+            blocks(source(dc, du))
+        for k in range(CHUNKS):
+            at = slice(k * step, (k + 1) * step)
+            total = total_out[at, :]
+            for du in range(n_sub):
+                slot = source(dc, du)
+                if du > 0:
+                    arrived(panel.at[slot, at], d_recv.at[dc, du, k])
+                total = total + term(slot, at)
+            line = potential[pl.ds(row * rb + k, 1), :]
+            row_pot = jnp.sum(jnp.where(eye, line, 0.0), axis=1, keepdims=True)
+            mine = panel[me, at, :].astype(F32)
+            coupled[at, :] = (total + COUPLE * (row_pot + col_pot) * mine).astype(BF16)
+
         arrived(hist.at[pl.ds(1, n_chip - 1)], h_send)
         arrived(field.at[pl.ds(1, n_chip - 1)], q_send)
         pl.when(target != me)(lambda: pass_inner(0).wait_send())
@@ -627,7 +633,7 @@
             pltpu.VMEM((neigh, waters), jnp.int32),
             pltpu.VMEM((n_m, rows, cols), BF16),
             pltpu.VMEM((n_row, rows + rb * cb, BLOCK), BF16),
-            pltpu.VMEM((rows, cols), BF16),
+            pltpu.VMEM((n_row, rows, cols), BF16),
             pltpu.VMEM((rows, cols), F32),
             pltpu.VMEM((wt, neigh // 8, 9, 8, BLOCK), F32),
             pltpu.VMEM((n_chip, nb, BLOCK), jnp.int16),

time: 24.2 us -> 23.9 us (0.988)
  the two profiles are of different devices: /device:TPU:25 before, /device:TPU:29 now
where the time goes in v4:
time: 23.9 us; the launch traced here: 23.7 us
  Pallas kernels  23 us (96%)
  between operations  0.64 us (3%)
    pallas_call x1, Pallas kernels, shards(): call(*[pltpu.with_memory_space_constraint(x, pltpu.HBM) for x in (density...  22.2 us
    pallas_call x1, Pallas kernels, deliver(): pl.pallas_call(kernel, out_shape=tuple((jax.ShapeDtypeStruct(r.shape, r.d...  0.85 us

profile of v4, /device:TPU:29, one launch (start us, length us, event | category | flops | bytes accessed | tf_op | source)
XLA Modules:
  0.0 23.7 jit_solution(8805753545457171166)
XLA Ops:
  0.6 22.2 %shard_map.155 = (bf16[512,512]{1,0:T(8,128)(2,1)S(1)}, f32[3,1024]{1,0:T(4,128)S(1)}, f32[3,1024]{1,0:T(4,128)S(1)}, f32[3,1024]{1,0:T(4,128)S(1)}, f32[4,1024]{1,0:T(4,128)S(1)}) custom-call(bf16[512,512]{1,0:T(8,128)(2,1)} %density_hbm.1, bf16[512,512]{1,0:T(8,128)(2,1)} %margin_hbm.1, s32[4,4]{1,0:T(4,128)} %pat_d_hbm.1, s32[4,4]{1,0:T(4,128)} %pat_s_hbm.1, ...), custom_call_target="tpu_custom_call" | custom-call | tf_op jit(solution)/shard_map/pallas_call | solution.py:697
  22.8 0.8 %shard_map.156 = (bf16[512,512]{1,0:T(8,128)(2,1)}, f32[3,1024]{1,0:T(4,128)}, f32[3,1024]{1,0:T(4,128)}, f32[3,1024]{1,0:T(4,128)}, f32[4,1024]{1,0:T(4,128)}) custom-call(bf16[512,512]{1,0:T(8,128)(2,1)S(1)} %get-tuple-element.10.refs_0_, f32[3,1024]{1,0:T(4,128)S(1)} %get-tuple-element.11.refs_1_, f32[3,1024]{1,0:T(4,128)S(1)} %get-tuple-element.12.refs_2_, ...), custom_call_target="tpu_custom_call" | custom-call | tf_op jit(solution)/shard_map/pallas_call | solution.py:678

commit v5 on v4

--- a/solution.py
+++ b/solution.py
@@ -318,6 +318,18 @@
                 halo_out[side, t * nh : (t + 1) * nh, :] = value[side * nh : (side + 1) * nh, :]
         in_all()
 
+        total = hist1[0].astype(jnp.int32)
+        for du in range(1, n_sub):
+            arrived(hist1.at[du], i_recv.at[du])
+            total = total + hist1[du].astype(jnp.int32)
+        hist[0] = total.astype(jnp.int16)
+
+        def share(q, carry):
+            remote(hist.at[0], hist.at[q], h_send, h_recv, chip(q)).start()
+            return carry
+
+        lax.fori_loop(1, n_chip, share, 0)
+
         def pass_inner(dr):
             there = peer_row(dr)
             there["col"], there["sub"] = lax.div(target, n_sub), lax.rem(target, n_sub)
@@ -337,17 +349,6 @@
                 send(halo_out.at[side], halo_in.at[side], e_send.at[side], e_recv.at[side],
                      peer_row(by))
             )
-        total = hist1[0].astype(jnp.int32)
-        for du in range(1, n_sub):
-            arrived(hist1.at[du], i_recv.at[du])
-            total = total + hist1[du].astype(jnp.int32)
-        hist[0] = total.astype(jnp.int16)
-
-        def share(q, carry):
-            remote(hist.at[0], hist.at[q], h_send, h_recv, chip(q)).start()
-            return carry
-
-        lax.fori_loop(1, n_chip, share, 0)
 
         def pass_block(to):
             return remote(
@@ -469,7 +470,6 @@
             )
         for side in range(2):
             arrived(halo_in.at[side], e_recv.at[side])
-        lax.fori_loop(0, wt // 4, pair_tile, 0)
         for du in range(1, n_sub):
             arrived(field1.at[du], g_recv.at[du])
             local = local + field1[du]
@@ -483,7 +483,7 @@
         pass_blocks(False)
         send_panels(6, CHUNKS + 2)
         pass_on(0)
-        lax.fori_loop(wt // 4, wt, pair_tile, 0)
+        lax.fori_loop(0, wt, pair_tile, 0)
         pass_on(1)
 
         col_pot = jnp.concatenate(
@@ -511,6 +511,22 @@
                 expand(r)
 
         pass_on(2)
+        pass_on(3)
+        flip = lax.rem(upper + lax.div(col, n_col // 2), 2)
+        for p in range(n_col - 1):
+            dc = lax.rem(p + flip, n_col)
+            for du in range(n_sub):
+                slot = source(dc, du)
+                if du > 0:
+                    for k in range(CHUNKS):
+                        arrived(panel.at[slot, pl.ds(k * step, step)], d_recv.at[dc, du, k])
+                blocks(slot)
+                for q in range(SPLIT):
+                    at = slice(q * rows // SPLIT, (q + 1) * rows // SPLIT)
+                    if p + du == 0:
+                        total_out[at, :] = term(slot, at)
+                    else:
+                        total_out[at, :] += term(slot, at)
         arrived(field.at[pl.ds(1, n_chip - 1)], q_recv)
         small[8].wait()
         small[9].wait()
@@ -558,22 +574,6 @@
         for c in range(4):
             spread(orient_new, c, moved[c] / length)
 
-        pass_on(3)
-        flip = lax.rem(upper + lax.div(col, n_col // 2), 2)
-        for p in range(n_col - 1):
-            dc = lax.rem(p + flip, n_col)
-            for du in range(n_sub):
-                slot = source(dc, du)
-                if du > 0:
-                    for k in range(CHUNKS):
-                        arrived(panel.at[slot, pl.ds(k * step, step)], d_recv.at[dc, du, k])
-                blocks(slot)
-                for q in range(SPLIT):
-                    at = slice(q * rows // SPLIT, (q + 1) * rows // SPLIT)
-                    if p + du == 0:
-                        total_out[at, :] = term(slot, at)
-                    else:
-                        total_out[at, :] += term(slot, at)
         dc = lax.rem(n_col - 1 + flip, n_col)
         for du in range(n_sub):
             blocks(source(dc, du))

time: 23.9 us -> 23.6 us (0.987)
  Pallas kernels: 23 us -> 22.7 us
    pallas_call x1, Pallas kernels: 22.2 us -> 21.8 us  [shards(): call(*[pltpu.with_memory_space_constraint(x, pltpu.HBM) for x in (density...]
where the time goes in v5:
time: 23.6 us; the launch traced here: 23.3 us
  Pallas kernels  22.7 us (96%)
  between operations  0.64 us (3%)
    pallas_call x1, Pallas kernels, shards(): call(*[pltpu.with_memory_space_constraint(x, pltpu.HBM) for x in (density...  21.8 us
    pallas_call x1, Pallas kernels, deliver(): pl.pallas_call(kernel, out_shape=tuple((jax.ShapeDtypeStruct(r.shape, r.d...  0.85 us

profile of v5, /device:TPU:29, one launch (start us, length us, event | category | flops | bytes accessed | tf_op | source)
XLA Modules:
  0.0 23.3 jit_solution(16131798643706555468)
XLA Ops:
  0.6 21.8 %shard_map.155 = (bf16[512,512]{1,0:T(8,128)(2,1)S(1)}, f32[3,1024]{1,0:T(4,128)S(1)}, f32[3,1024]{1,0:T(4,128)S(1)}, f32[3,1024]{1,0:T(4,128)S(1)}, f32[4,1024]{1,0:T(4,128)S(1)}) custom-call(bf16[512,512]{1,0:T(8,128)(2,1)} %density_hbm.1, bf16[512,512]{1,0:T(8,128)(2,1)} %margin_hbm.1, s32[4,4]{1,0:T(4,128)} %pat_d_hbm.1, s32[4,4]{1,0:T(4,128)} %pat_s_hbm.1, ...), custom_call_target="tpu_custom_call" | custom-call | tf_op jit(solution)/shard_map/pallas_call | solution.py:697
  22.5 0.8 %shard_map.156 = (bf16[512,512]{1,0:T(8,128)(2,1)}, f32[3,1024]{1,0:T(4,128)}, f32[3,1024]{1,0:T(4,128)}, f32[3,1024]{1,0:T(4,128)}, f32[4,1024]{1,0:T(4,128)}) custom-call(bf16[512,512]{1,0:T(8,128)(2,1)S(1)} %get-tuple-element.10.refs_0_, f32[3,1024]{1,0:T(4,128)S(1)} %get-tuple-element.11.refs_1_, f32[3,1024]{1,0:T(4,128)S(1)} %get-tuple-element.12.refs_2_, ...), custom_call_target="tpu_custom_call" | custom-call | tf_op jit(solution)/shard_map/pallas_call | solution.py:678

commit v6 on v5

--- a/solution.py
+++ b/solution.py
@@ -462,18 +462,7 @@
             weigh = COUPLE * potential[pl.ds(row * rb + i, 1), :]
             inner2 = got[0:3, :] + got[3:6, :] + weigh * got[6:9, :]
             low_u[i] = jnp.concatenate([inner2, jnp.zeros((1, BLOCK), F32)], axis=0)
-        local = jnp.concatenate(low_u, axis=0)
-        field1[0] = local
-        for du in range(1, n_sub):
-            started.append(
-                send(field1.at[0], field1.at[du], g_send.at[du], g_recv.at[du], peer(0, du))
-            )
-        for side in range(2):
-            arrived(halo_in.at[side], e_recv.at[side])
-        for du in range(1, n_sub):
-            arrived(field1.at[du], g_recv.at[du])
-            local = local + field1[du]
-        field[0] = local.astype(BF16)
+        field[0] = jnp.concatenate(low_u, axis=0).astype(BF16)
 
         def tell(q, carry):
             remote(field.at[0], field.at[q], q_send, q_recv, chip(q)).start()
@@ -483,6 +472,8 @@
         pass_blocks(False)
         send_panels(6, CHUNKS + 2)
         pass_on(0)
+        for side in range(2):
+            arrived(halo_in.at[side], e_recv.at[side])
         lax.fori_loop(0, wt, pair_tile, 0)
         pass_on(1)
 
@@ -511,6 +502,16 @@
                 expand(r)
 
         pass_on(2)
+        arrived(field.at[pl.ds(1, n_chip - 1)], q_recv)
+        for dr in range(n_row):
+            total = field[dr * n_col].astype(F32)
+            for m in range(1, n_col):
+                total = total + field[dr * n_col + m].astype(F32)
+            field1[0, lax.rem(row + n_row - dr, n_row)] = total
+        for du in range(1, n_sub):
+            started.append(
+                send(field1.at[0], field1.at[du], g_send.at[du], g_recv.at[du], peer(0, du))
+            )
         pass_on(3)
         flip = lax.rem(upper + lax.div(col, n_col // 2), 2)
         for p in range(n_col - 1):
@@ -527,14 +528,15 @@
                         total_out[at, :] = term(slot, at)
                     else:
                         total_out[at, :] += term(slot, at)
-        arrived(field.at[pl.ds(1, n_chip - 1)], q_recv)
         small[8].wait()
         small[9].wait()
-        for dr in range(n_row):
-            total = field[dr * n_col].astype(F32)
-            for m in range(1, n_col):
-                total = total + field[dr * n_col + m].astype(F32)
-            sums[lax.rem(row + n_row - dr, n_row)] = total
+        for du in range(1, n_sub):
+            arrived(field1.at[du], g_recv.at[du])
+        for r in range(n_row):
+            total = field1[0, r]
+            for du in range(1, n_sub):
+                total = total + field1[du, r]
+            sums[r] = total
 
         forces = []
         for a in range(3):
@@ -648,7 +650,7 @@
             pltpu.VMEM((nb, BLOCK), F32),
             pltpu.VMEM((n_row, rb * 4, BLOCK), F32),
             pltpu.VMEM((n_sub, nb, BLOCK), jnp.int16),
-            pltpu.VMEM((n_sub, rb * 4, BLOCK), F32),
+            pltpu.VMEM((n_sub, n_row, rb * 4, BLOCK), F32),
             dma(11), dma(CHUNKS),
             dma(n_col, n_sub, CHUNKS), dma(n_col, n_sub, CHUNKS), dma(n_col, n_sub, CHUNKS),
             dma(n_row), dma(n_row), one, one, dma(n_row), dma(wide, n_m),

time: 23.6 us -> 23.5 us (level)
  the two profiles are of different devices: /device:TPU:29 before, /device:TPU:0 now
where the time goes in v6:
time: 23.5 us; the launch traced here: 23.2 us
  Pallas kernels  22.6 us (96%)
  between operations  0.64 us (3%)
    pallas_call x1, Pallas kernels, shards(): call(*[pltpu.with_memory_space_constraint(x, pltpu.HBM) for x in (density...  21.7 us
    pallas_call x1, Pallas kernels, deliver(): pl.pallas_call(kernel, out_shape=tuple((jax.ShapeDtypeStruct(r.shape, r.d...  0.85 us

profile of v6, /device:TPU:0, one launch (start us, length us, event | category | flops | bytes accessed | tf_op | source)
XLA Modules:
  0.0 23.2 jit_solution(15992944143649983818)
XLA Ops:
  0.6 21.7 %shard_map.155 = (bf16[512,512]{1,0:T(8,128)(2,1)S(1)}, f32[3,1024]{1,0:T(4,128)S(1)}, f32[3,1024]{1,0:T(4,128)S(1)}, f32[3,1024]{1,0:T(4,128)S(1)}, f32[4,1024]{1,0:T(4,128)S(1)}) custom-call(bf16[512,512]{1,0:T(8,128)(2,1)} %density_hbm.1, bf16[512,512]{1,0:T(8,128)(2,1)} %margin_hbm.1, s32[4,4]{1,0:T(4,128)} %pat_d_hbm.1, s32[4,4]{1,0:T(4,128)} %pat_s_hbm.1, ...), custom_call_target="tpu_custom_call" | custom-call | tf_op jit(solution)/shard_map/pallas_call | solution.py:699
  22.4 0.8 %shard_map.156 = (bf16[512,512]{1,0:T(8,128)(2,1)}, f32[3,1024]{1,0:T(4,128)}, f32[3,1024]{1,0:T(4,128)}, f32[3,1024]{1,0:T(4,128)}, f32[4,1024]{1,0:T(4,128)}) custom-call(bf16[512,512]{1,0:T(8,128)(2,1)S(1)} %get-tuple-element.10.refs_0_, f32[3,1024]{1,0:T(4,128)S(1)} %get-tuple-element.11.refs_1_, f32[3,1024]{1,0:T(4,128)S(1)} %get-tuple-element.12.refs_2_, ...), custom_call_target="tpu_custom_call" | custom-call | tf_op jit(solution)/shard_map/pallas_call | solution.py:680

commit v7 on v6

--- a/solution.py
+++ b/solution.py
@@ -365,7 +365,7 @@
                 pl.when(jnp.logical_and(row != to, go))(lambda to=to: pass_block(to).start())
 
         pass_blocks(True)
-        send_panels(2, 6)
+        send_panels(2, 5)
         def expand(r):
             marks = comp[r, rows : rows + rb * cb, :].astype(F32)
             for i in range(rb):
@@ -470,7 +470,7 @@
 
         lax.fori_loop(1, n_chip, tell, 0)
         pass_blocks(False)
-        send_panels(6, CHUNKS + 2)
+        send_panels(5, CHUNKS + 2)
         pass_on(0)
         for side in range(2):
             arrived(halo_in.at[side], e_recv.at[side])

time: 23.5 us -> 23.4 us (level)
  no operation moved by 1% of the time
where the time goes in v7:
time: 23.4 us; the launch traced here: 23.2 us
  Pallas kernels  22.6 us (97%)
  between operations  0.64 us (3%)
    pallas_call x1, Pallas kernels, shards(): call(*[pltpu.with_memory_space_constraint(x, pltpu.HBM) for x in (density...  21.7 us
    pallas_call x1, Pallas kernels, deliver(): pl.pallas_call(kernel, out_shape=tuple((jax.ShapeDtypeStruct(r.shape, r.d...  0.85 us

profile of v7, /device:TPU:0, one launch (start us, length us, event | category | flops | bytes accessed | tf_op | source)
XLA Modules:
  0.0 23.2 jit_solution(18312750267736924144)
XLA Ops:
  0.6 21.7 %shard_map.155 = (bf16[512,512]{1,0:T(8,128)(2,1)S(1)}, f32[3,1024]{1,0:T(4,128)S(1)}, f32[3,1024]{1,0:T(4,128)S(1)}, f32[3,1024]{1,0:T(4,128)S(1)}, f32[4,1024]{1,0:T(4,128)S(1)}) custom-call(bf16[512,512]{1,0:T(8,128)(2,1)} %density_hbm.1, bf16[512,512]{1,0:T(8,128)(2,1)} %margin_hbm.1, s32[4,4]{1,0:T(4,128)} %pat_d_hbm.1, s32[4,4]{1,0:T(4,128)} %pat_s_hbm.1, ...), custom_call_target="tpu_custom_call" | custom-call | tf_op jit(solution)/shard_map/pallas_call | solution.py:699
  22.4 0.8 %shard_map.156 = (bf16[512,512]{1,0:T(8,128)(2,1)}, f32[3,1024]{1,0:T(4,128)}, f32[3,1024]{1,0:T(4,128)}, f32[3,1024]{1,0:T(4,128)}, f32[4,1024]{1,0:T(4,128)}) custom-call(bf16[512,512]{1,0:T(8,128)(2,1)S(1)} %get-tuple-element.10.refs_0_, f32[3,1024]{1,0:T(4,128)S(1)} %get-tuple-element.11.refs_1_, f32[3,1024]{1,0:T(4,128)S(1)} %get-tuple-element.12.refs_2_, ...), custom_call_target="tpu_custom_call" | custom-call | tf_op jit(solution)/shard_map/pallas_call | solution.py:680
